TPU v7x, 32 devices: a whole 2x2x4 slice. The times are simulated.
32 devices in a mesh: groups: 2 (over y), aux: 4 (over z), row: 4 (over x, core).
Axes of the slice: x: 2, y: 2, z: 4, core: 2. Of those that a mesh axis runs over, the one named last changes fastest.
Arguments:
- tensor_tiles: bfloat16 [64, 96, 128, 128], P(('groups', 'aux'), 'row'), parts along dimension 0, may hold values from -6 to 6
- pair_rows: int32 [8, 96], P(('groups', 'aux'), 'row'), parts along dimension 0, may hold values from 0 to 15, as said below
- pair_cols: int32 [8, 96], P(('groups', 'aux'), 'row'), parts along dimension 0, may hold values from 0 to 63
- live_count: int32 [8, 4], P(('groups', 'aux'), 'row'), parts along dimension 0, may hold values from 16 to 24, as said below
- orbitals: bfloat16 [8192, 512], P(None, 'groups'), parts along dimension 1, may hold values from -0.375 to 0.375
- metric: bfloat16 [32, 32], replicated, as said below
Outputs:
- exchange: float32 [1024, 8192], P(('groups', 'aux'), 'row'), parts along dimension 0
There are 2 independent parts, one for each index of `groups`. A program takes and returns all parts, laid end to end along the dimension named above; an argument that names none is the same for every part. Nothing has to cross between parts.
Inputs may be any that keep to these rules, and one draw needn't show every extreme that they name: `pair_rows`: slot t < 16 of every device holds p shell block t. `live_count`: some device has all 24 slots live. `metric`: symmetric.
All inputs are finite; a program needn't handle non-finite values.
Results may differ from a plain program's by a relative error of at most 0.0043.
Values may be sent and summed in bfloat16 or wider, within the bound.
No kernel may reach another device: no remote copies, remote signals or barrier semaphores. Data moves between devices by JAX's collectives and lax.ppermute only.
A program may use at most 128 MiB of HBM per device.

v0:
```python
import jax
import jax.numpy as jnp
from jax import lax
from jax.sharding import PartitionSpec as P

KR = 128


def shards(tensor_tiles, pair_rows, pair_cols, live_count, orbitals, metric):
    aux_dev, slot_count, block_width, _ = tensor_tiles.shape
    basis_count, occ_count = orbitals.shape
    blocks_dev = basis_count // (block_width * lax.axis_size("row"))
    rows_dev = blocks_dev * block_width
    column_rows = orbitals.reshape(basis_count // block_width, block_width, occ_count)[pair_cols[0]]
    live_limit = live_count[0, 0]
    active = jnp.arange(slot_count, dtype=jnp.int32) < live_limit
    placing = (
        (pair_rows[0][:, None] == jnp.arange(blocks_dev, dtype=jnp.int32)[None, :])
        & active[:, None]
    ).astype(jnp.float32)
    partial_value = jnp.einsum(
        "qtps,tsi->tqip", tensor_tiles, column_rows, preferred_element_type=jnp.float32
    )
    summed = jnp.einsum("tb,tqip->qibp", placing, partial_value, precision=lax.Precision.HIGHEST)
    half_tensor = summed.reshape(aux_dev, occ_count, rows_dev).astype(jnp.bfloat16)
    exchanged = lax.all_to_all(half_tensor, "aux", split_axis=1, concat_axis=0, tiled=True)
    flattened = exchanged.reshape(exchanged.shape[0], -1)
    product = jnp.dot(metric, flattened, preferred_element_type=jnp.float32)
    fitted = product.astype(jnp.bfloat16).reshape(exchanged.shape)
    window = fitted[:, :, :KR]
    rows_all = lax.all_gather(window, "row", axis=2, tiled=True)
    left_side = rows_all.reshape(-1, rows_all.shape[2])
    right_side = fitted.reshape(-1, rows_dev)
    row_share = left_side.shape[1] // lax.axis_size("aux")
    summed_all = lax.psum(
        lax.dot_general(
            left_side, right_side, (((0,), (0,)), ((), ())), preferred_element_type=jnp.float32
        ),
        "aux",
    )
    result = lax.dynamic_slice_in_dim(summed_all, lax.axis_index("aux") * row_share, row_share, 0)
    return result


def solution(mesh):
    return jax.shard_map(
        shards,
        mesh=mesh,
        in_specs=(
            P(("groups", "aux"), "row", None, None),
            P(("groups", "aux"), "row"),
            P(("groups", "aux"), "row"),
            P(("groups", "aux"), "row"),
            P(None, "groups"),
            P(),
        ),
        out_specs=P(("groups", "aux"), "row"),
        check_vma=False,
    )
```

profile of v0, /device:TPU:0, one launch (start us, length us, event | category | flops | bytes accessed | tf_op | source)
XLA Modules:
  0.0 485.3 jit_solution(3890940190820778181)
XLA Ops:
  6.5 0.0 copy-start
  6.5 0.0 all-gather.2.cloned.1.call-start
  6.5 0.7 fusion.11
  7.9 2.8 gather_fusion
  10.7 0.0 copy-start.1
  10.7 12.9 %convolution_bitcast_fusion = f32[24,8,256,128]{3,2,1,0:T(8,128)} fusion(bf16[8,24,128,128]{3,2,1,0:T(8,128)(2,1)} %param.6, bf16[24,128,256]{2,1,0:T(8,128)(2,1)S(1)} %gather_fusion), kind=kOutput, calls=%fused_computation.4 | convolution fusion | flops 1610612736 | bytes 33030144 | tf_op jit(solution)/shard_map/qtps,tsi->tqip/dot_general | solution.py:21
  23.7 0.0 copy-done.1
  23.7 31.4 %convert_bitcast_fusion = bf16[8,256,16,128]{3,2,1,0:T(8,128)(2,1)} fusion(f32[24,8,256,128]{3,2,1,0:T(8,128)} %convolution_bitcast_fusion, s32[24]{0:T(128)S(1)} %bitcast.42, pred[24]{0:T(512)(128)(4,1)S(1)} %iota_compare_fusion.1), kind=kOutput, calls=%fused_computation.5 | convolution fusion | flops 1212154624 | bytes 33554552 | tf_op jit(solution)/shard_map/tb,tqip->qibp/dot_general | solution.py:24
  55.1 13.3 %convert_element_type.18 = bf16[8,256,2048]{2,1,0:T(8,128)(2,1)} reshape(bf16[8,256,16,128]{3,2,1,0:T(8,128)(2,1)} %convert_bitcast_fusion) | data formatting | bytes 16777216 | tf_op jit(solution)/shard_map/convert_element_type | solution.py:25
  68.4 11.2 %copy.17 = bf16[8,256,2048]{2,0,1:T(8,128)(2,1)} copy(bf16[8,256,2048]{2,1,0:T(8,128)(2,1)} %convert_element_type.18) | data formatting | bytes 16777216 | tf_op jit(solution)/shard_map/convert_element_type | solution.py:25
  79.6 189.3 %all_to_all.15 = bf16[8,256,2048]{2,0,1:T(8,128)(2,1)S(1)} all-to-all(bf16[8,256,2048]{2,0,1:T(8,128)(2,1)} %copy.17), channel_id=1, replica_groups=mesh['groups'=2,'aux'=4,'row'=4] {'aux'}, dimensions={1} | all-to-all | bytes 16777216 | tf_op jit(solution)/shard_map/all_to_all | solution.py:26
  269.0 0.0 copy-done
  269.0 5.6 %convolution_convert_fusion = bf16[131072,32]{0,1:T(8,128)(2,1)} fusion(bf16[32,32]{1,0:T(8,128)(2,1)S(1)} %copy-done, bf16[32,131072]{1,0:T(8,128)(2,1)S(1)} %bitcast.39), kind=kOutput, calls=%fused_computation.1 | convolution fusion | flops 272629760 | bytes 16779264 | tf_op jit(solution)/shard_map/dot_general | solution.py:28
  274.5 11.4 %copy.25 = bf16[4,8,64,2048]{3,2,1,0:T(8,128)(2,1)} copy(bf16[4,8,64,2048]{3,1,2,0:T(8,128)(2,1)} %bitcast.37) | data formatting | bytes 16777216
  285.9 1.9 slice.6
  287.8 0.0 all-gather.2.cloned.1.call-update
  287.8 0.0 all-reduce.2.cloned.1.call-start
  287.8 9.1 %reshape_reshape.3 = bf16[2048,2048]{1,0:T(8,128)(2,1)} reshape(bf16[32,131072]{1,0:T(8,128)(2,1)} %bitcast.38) | data formatting | bytes 16777216 | tf_op jit(solution)/shard_map/reshape;reshape | solution.py:33
  297.0 13.5 %all-gather.2.cloned.1.call-done = bf16[32,64,512]{2,1,0:T(8,128)(2,1)} async-done(((bf16[32,64,128]{2,1,0:T(8,128)(2,1)}), bf16[32,64,512]{2,1,0:T(8,128)(2,1)}) %all-gather.2.cloned.1.call-update) | async-done | bytes 2097168 | tf_op jit(solution)/shard_map/all_gather | solution.py:31
  310.4 10.5 %fusion.12 = f32[512,2048]{1,0:T(8,128)} fusion(bf16[2048,512]{1,0:T(8,128)(2,1)} %bitcast.43, bf16[2048,2048]{1,0:T(8,128)(2,1)} %reshape_reshape.3), kind=kOutput, calls=%fused_computation.18 | convolution fusion | flops 4294967296 | bytes 14680064 | tf_op jit(solution)/shard_map/dot_general | solution.py:36
  321.0 0.0 all-reduce.2.cloned.1.call-update
  321.0 155.1 %all-reduce.2.cloned.1.call-done = f32[512,2048]{1,0:T(8,128)} async-done(((f32[512,2048]{1,0:T(8,128)}), f32[512,2048]{1,0:T(8,128)}) %all-reduce.2.cloned.1.call-update) | async-done | bytes 4194320 | tf_op jit(solution)/shard_map/psum | solution.py:35
  476.1 2.3 constant_dynamic-slice_fusion
  (2 shorter events, 0.0 us)
Async XLA Ops:
  6.5 262.4 %copy-start = (bf16[32,32]{1,0:T(8,128)(2,1)S(1)}, bf16[32,32]{1,0:T(8,128)(2,1)}, u32[]{:S(2)}) copy-start(bf16[32,32]{1,0:T(8,128)(2,1)} %param.11) | copy-start | bytes 6148
  6.5 303.9 %all-gather.2.cloned.1.call-start = ((), (), s32[]{:S(2)}) async-start(), calls=%async_computation.1 | async-start | bytes 2621440 | tf_op jit(solution)/shard_map/all_gather | solution.py:31
  10.7 12.9 %copy-start.1 = (s32[1,24]{1,0:T(1,128)S(1)}, s32[1,24]{1,0:T(1,128)}, u32[]{:S(2)}) copy-start(s32[1,24]{1,0:T(1,128)} %param.7) | copy-start | bytes 292
  287.8 188.3 %all-reduce.2.cloned.1.call-start = ((), (), s32[]{:S(2)}) async-start(), calls=%async_computation.2 | async-start | bytes 8388608 | tf_op jit(solution)/shard_map/psum | solution.py:35
Sparse Core Ops, SparseCore 0:
  287.9 22.4 all-gather.1
  321.1 154.9 all-reduce.1
where the time goes:
time: 486 us; the launch traced here: 485 us
  blocking collectives  189 us (39%)
  waiting for transfers between devices  169 us (35%)
  matrix products  60.4 us (12%)
  local copies, waits for them, and re-layouts  52 us (11%)
  between operations  14.1 us (3%)
    all_to_all x1, blocking collectives, shards(): lax.all_to_all(half_tensor, 'aux', split_axis=1, concat_axis=0, tiled=True)  189 us
    psum x1, waiting for transfers between devices, shards(): lax.psum(lax.dot_general(left_side, right_side, (((0,), (0,)), ((), ())),...  155 us
    dot_general x1, matrix products, shards(): jnp.einsum('tb,tqip->qibp', placing, partial_value, precision=lax.Precisi...  31.4 us
    convert_element_type x2, local copies, waits for them, and re-layouts, shards(): summed.reshape(aux_dev, occ_count, rows_dev).astype(jnp.bfloat16)  24.6 us
    all_gather x1, waiting for transfers between devices, shards(): rows_all = lax.all_gather(window, 'row', axis=2, tiled=True)  13.5 us
    dot_general x1, matrix products, shards(): jnp.einsum('qtps,tsi->tqip', tensor_tiles, column_rows, preferred_element...  12.9 us
    unnamed x5, local copies, waits for them, and re-layouts  11.4 us
    dot_general x1, matrix products, shards(): lax.dot_general(left_side, right_side, (((0,), (0,)), ((), ())), preferre...  10.5 us
  transfers between devices with their start and end apart: 2, of which 2 were waited for; matrix products, arithmetic and copies ran while one was open for 2% of the time, Pallas kernels for 0%

commit v1 on v0

v1 whole, which is shorter than its diff:
```python
import functools

import jax
import jax.numpy as jnp
from jax import lax
from jax.experimental import pallas as pl
from jax.experimental.pallas import tpu as pltpu
from jax.sharding import PartitionSpec as P

KR = 128
HALVES = 2
LIMIT = 48 * 1024 * 1024
F32 = jnp.float32
BF16 = jnp.bfloat16


def half_body(first, blocks, extras, outs, rows, cols, live, tile, more, orb, *rest):
    orbs, out_refs, acc = rest[:extras], rest[extras:extras + outs], rest[-1]
    aux_dev, _, width, _ = tile.shape
    occ = orb.shape[1]
    block = pl.program_id(0) + first
    for q in range(aux_dev):
        acc[:, q * occ:(q + 1) * occ] = jnp.dot(tile[q, 0], orb[...], preferred_element_type=F32)
    for e in range(extras):
        @pl.when((rows[blocks + e] == block) & (blocks + e < live[0]))
        def _():
            for q in range(aux_dev):
                acc[:, q * occ:(q + 1) * occ] += jnp.dot(
                    more[q, e], orbs[e][...], preferred_element_type=F32)
    part = width // outs
    for k in range(outs):
        out_refs[k][...] = acc[k * part:(k + 1) * part, :].astype(BF16)


def half_rows(tiles, rows, cols, live, orbitals, first, count, outs):
    aux_dev, slots, width, _ = tiles.shape
    basis, occ = orbitals.shape
    blocks = basis // (width * lax.axis_size("row"))
    extras = slots - blocks
    wide = aux_dev * occ
    in_specs = [
        pl.BlockSpec((aux_dev, 1, width, width), lambda b, r, c, n: (0, b + first, 0, 0)),
        pl.BlockSpec((aux_dev, extras, width, width), lambda b, r, c, n: (0, blocks // extras, 0, 0)),
        pl.BlockSpec((width, occ), lambda b, r, c, n: (c[b + first], 0)),
    ]
    for e in range(extras):
        in_specs.append(pl.BlockSpec((width, occ), lambda b, r, c, n, e=e: (c[blocks + e], 0)))
    part = width // outs
    out = pl.pallas_call(
        functools.partial(half_body, first, blocks, extras, outs),
        grid_spec=pltpu.PrefetchScalarGridSpec(
            num_scalar_prefetch=3,
            grid=(count,),
            in_specs=in_specs,
            out_specs=[pl.BlockSpec((part, wide), lambda b, r, c, n: (b, 0))] * outs,
            scratch_shapes=[pltpu.VMEM((width, wide), F32)],
        ),
        out_shape=[jax.ShapeDtypeStruct((count * part, wide), BF16)] * outs,
        compiler_params=pltpu.CompilerParams(vmem_limit_bytes=LIMIT),
        cost_estimate=pl.CostEstimate(
            flops=4 * count * width * wide * width,
            bytes_accessed=2 * (count * (aux_dev * width * width + width * wide) + aux_dev * extras * width * width),
            transcendentals=0),
    )(rows, cols, live, tiles, tiles, *([orbitals] * (1 + extras)))
    return out


def mix_body(occ, weight, near, far, out):
    outs_q = out.shape[1] // occ
    ins_q = near.shape[1] // occ
    step = 16

    def chunk(c, carry):
        span = pl.ds(pl.multiple_of(c * step, step), step)
        sums = [None] * outs_q
        for k in range(2 * ins_q):
            ref, q = (near, k) if k < ins_q else (far, k - ins_q)
            x = ref[span, q * occ:(q + 1) * occ].astype(F32)
            for p in range(outs_q):
                term = x * weight[p, k]
                sums[p] = term if sums[p] is None else sums[p] + term
        for p in range(outs_q):
            out[span, p * occ:(p + 1) * occ] = sums[p].astype(out.dtype)
        return carry

    lax.fori_loop(0, near.shape[0] // step, chunk, 0)


def mix(weight, near, far, occ, dtype):
    rows, wide = near.shape
    return pl.pallas_call(
        functools.partial(mix_body, occ),
        in_specs=[pl.BlockSpec(memory_space=pltpu.SMEM)] + [pl.BlockSpec(memory_space=pltpu.VMEM)] * 2,
        out_specs=pl.BlockSpec(memory_space=pltpu.VMEM),
        out_shape=jax.ShapeDtypeStruct((rows, wide), dtype),
        compiler_params=pltpu.CompilerParams(vmem_limit_bytes=LIMIT),
        cost_estimate=pl.CostEstimate(
            flops=2 * rows * wide * weight.shape[1] * 100, bytes_accessed=8 * rows * wide, transcendentals=0),
    )(weight, near, far)


def product_body(places, *refs):
    pieces, right, send, near, own, left = refs[:4], refs[4], refs[5], refs[6], refs[7], refs[8]
    rows = pieces[0].shape[0]

    @pl.when(pl.program_id(0) == 0)
    def _():
        for k in range(4):
            left[pl.ds(pl.multiple_of(places[k] * rows, rows), rows), :] = pieces[k][...]

    product = lax.dot_general(
        left[...], right[...], (((1,), (1,)), ((), ())), preferred_element_type=F32)
    send[...] = product[:2 * rows].astype(BF16)
    near[...] = product[2 * rows:3 * rows]
    own[...] = product[3 * rows:]


def product_rows(places, pieces, right):
    rows, wide = pieces[0].shape
    count = right.shape[0]
    step = 512
    whole = pl.BlockSpec((rows, wide), lambda n, s: (0, 0))
    return pl.pallas_call(
        product_body,
        grid_spec=pltpu.PrefetchScalarGridSpec(
            num_scalar_prefetch=1,
            grid=(count // step,),
            in_specs=[whole] * 4 + [pl.BlockSpec((step, wide), lambda n, s: (n, 0))],
            out_specs=[
                pl.BlockSpec((2 * rows, step), lambda n, s: (0, n)),
                pl.BlockSpec((rows, step), lambda n, s: (0, n)),
                pl.BlockSpec((rows, step), lambda n, s: (0, n)),
            ],
            scratch_shapes=[pltpu.VMEM((4 * rows, wide), BF16)],
        ),
        out_shape=[
            jax.ShapeDtypeStruct((2 * rows, count), BF16),
            jax.ShapeDtypeStruct((rows, count), F32),
            jax.ShapeDtypeStruct((rows, count), F32),
        ],
        compiler_params=pltpu.CompilerParams(vmem_limit_bytes=LIMIT),
        cost_estimate=pl.CostEstimate(
            flops=8 * rows * wide * count, bytes_accessed=2 * wide * (count + 4 * rows), transcendentals=0),
    )(places, *pieces, right)


def swap(x, axis, distance):
    size = lax.axis_size(axis)
    return lax.ppermute(x, axis, [(i, i ^ distance) for i in range(size)])


def four_by_four(window, right, squared, aux_dev, occ):
    z, r = lax.axis_index("aux"), lax.axis_index("row")
    table = squared.reshape(4, aux_dev, 4, aux_dev)
    pick = lambda p, q: table[p, :, q, :]
    weights = [jnp.concatenate([pick(p, z), pick(p, z ^ 2)], axis=1) for p in (z ^ 1, z)]
    place = jnp.array([3, 0, 2, 1], jnp.int32)
    places = place[(r ^ jnp.arange(4, dtype=jnp.int32)) ^ z]
    results = []
    for x in window:
        far = swap(x, "aux", 2)
        message = swap(mix(weights[0], x, far, occ, BF16), "aux", 1)
        mine = mix(weights[1], x, far, occ, F32)
        g0 = (mine + message.astype(F32)).astype(BF16)
        g2 = swap(g0, "row", 2)
        g1 = swap(g0, "row", 1)
        g3 = swap(g2, "row", 1)
        send, near, own = product_rows(places, (g0, g1, g2, g3), right)
        rows = near.shape[0]
        came = swap(send, "aux", 1)
        passed = swap((near + came[rows:].astype(F32)).astype(BF16), "aux", 2)
        results.append(own + came[:rows].astype(F32) + passed.astype(F32))
    return jnp.concatenate(results, axis=0)


def any_mesh(window, right, squared, aux_dev, occ):
    rows = window.shape[0]
    aux = lax.axis_size("aux")
    gathered = lax.all_gather(window, "aux", axis=0, tiled=True).reshape(aux, rows, aux_dev, occ)
    own = lax.dynamic_slice_in_dim(squared, lax.axis_index("aux") * aux_dev, aux_dev, 0)
    own = own.reshape(aux_dev, aux, aux_dev)
    mixed = jnp.einsum("paq,amqi->mpi", own, gathered.astype(F32), precision=lax.Precision.HIGHEST)
    left = lax.all_gather(mixed.astype(BF16).reshape(rows, -1), "row", axis=0, tiled=True)
    product = lax.dot_general(left, right, (((1,), (1,)), ((), ())), preferred_element_type=F32)
    return lax.psum_scatter(product, "aux", scatter_dimension=0, tiled=True)


def shards(tensor_tiles, pair_rows, pair_cols, live_count, orbitals, metric):
    aux_dev, _, width, _ = tensor_tiles.shape
    basis, occ = orbitals.shape
    blocks = basis // (width * lax.axis_size("row"))
    shape44 = lax.axis_size("aux") == 4 and lax.axis_size("row") == 4
    squared = jnp.dot(metric.T, metric, preferred_element_type=F32)
    halves = functools.partial(
        half_rows, tensor_tiles, pair_rows[0], pair_cols[0], live_count[0], orbitals)
    window = halves(0, 1, HALVES if shape44 else 1)
    right, = halves(0, blocks, 1)
    if shape44:
        return four_by_four(window, right, squared, aux_dev, occ)
    return any_mesh(window[0], right, squared, aux_dev, occ)


def solution(mesh):
    return jax.shard_map(
        shards,
        mesh=mesh,
        in_specs=(
            P(("groups", "aux"), "row", None, None),
            P(("groups", "aux"), "row"),
            P(("groups", "aux"), "row"),
            P(("groups", "aux"), "row"),
            P(None, "groups"),
            P(),
        ),
        out_specs=P(("groups", "aux"), "row"),
        check_vma=False,
    )
```

time: 486 us -> 117 us (0.24)
  blocking collectives: 189 us -> 0 us
  waiting for transfers between devices: 169 us -> 58.6 us
  matrix products: 60.4 us -> 0.17 us
  local copies, waits for them, and re-layouts: 52 us -> 6.45 us
  Pallas kernels: 0 us -> 35.6 us
  between operations: 14.1 us -> 0.83 us
  starting transfers between devices: 0.04 us -> 13 us
    all_to_all x1 -> x0, blocking collectives: 189 us -> none  [shards(): lax.all_to_all(half_tensor, 'aux', split_axis=1, concat_axis=0, tiled=True)]
    psum x1 -> x0, waiting for transfers between devices: 155 us -> none  [shards(): lax.psum(lax.dot_general(left_side, right_side, (((0,), (0,)), ((), ())),...]
    dot_general x4 -> x1, matrix products: 60.4 us -> 0.17 us  [shards(): squared = jnp.dot(metric.T, metric, preferred_element_type=F32)]
    ppermute x0 -> x14, waiting for transfers between devices: none -> 58.6 us  [swap(): return lax.ppermute(x, axis, [(i, i ^ distance) for i in range(size)])]
    pallas_call x0 -> x8, Pallas kernels: none -> 35.6 us  [the longest x2 17.9 us: half_rows(): pl.pallas_call(functools.partial(half_body, first, blocks, extras, outs),...]
    convert_element_type x2 -> x0, local copies, waits for them, and re-layouts: 24.6 us -> none  [shards(): summed.reshape(aux_dev, occ_count, rows_dev).astype(jnp.bfloat16)]
    all_gather x1 -> x0, waiting for transfers between devices: 13.5 us -> none  [shards(): rows_all = lax.all_gather(window, 'row', axis=2, tiled=True)]
    ppermute x0 -> x14, starting transfers between devices: none -> 13 us  [swap(): return lax.ppermute(x, axis, [(i, i ^ distance) for i in range(size)])]
  transfers between devices with their start and end apart: 2 -> 14, of which waited for: 2 -> 10; matrix products, arithmetic and copies ran while one was open for 2% -> 1% of each run, Pallas kernels for 0% -> 28%
where the time goes in v1:
time: 117 us; the launch traced here: 116 us
  waiting for transfers between devices  58.6 us (50%)
  Pallas kernels  35.6 us (30%)
  starting transfers between devices  13 us (11%)
  local copies, waits for them, and re-layouts  6.45 us (6%)
  other arithmetic  1.6 us (1%)
    ppermute x14, waiting for transfers between devices, swap(): return lax.ppermute(x, axis, [(i, i ^ distance) for i in range(size)])  58.6 us
    pallas_call x2, Pallas kernels, half_rows(): pl.pallas_call(functools.partial(half_body, first, blocks, extras, outs),...  17.9 us
    ppermute x14, starting transfers between devices, swap(): return lax.ppermute(x, axis, [(i, i ^ distance) for i in range(size)])  13 us
    pallas_call x2, Pallas kernels, product_rows(): pl.pallas_call(product_body, grid_spec=pltpu.PrefetchScalarGridSpec(num_s...  12.6 us
    unnamed x16, local copies, waits for them, and re-layouts  5.69 us
    pallas_call x4, Pallas kernels, mix(): pl.pallas_call(functools.partial(mix_body, occ), in_specs=[pl.BlockSpec(m...  5.09 us
  transfers between devices with their start and end apart: 14, of which 10 were waited for; matrix products, arithmetic and copies ran while one was open for 1% of the time, Pallas kernels for 28%

profile of v1, /device:TPU:0, one launch (start us, length us, event | category | flops | bytes accessed | tf_op | source)
XLA Modules:
  0.0 116.2 jit_solution(71923369471785030)
XLA Ops:
  0.7 2.2 %copy-done.1 = bf16[8192,256]{1,0:T(8,128)(2,1)S(1)} copy-done((bf16[8192,256]{1,0:T(8,128)(2,1)S(1)}, bf16[8192,256]{1,0:T(8,128)(2,1)}, u32[]{:S(2)}) %copy-start.1) | copy-done | bytes 4194328
  4.2 2.6 %shard_map.73 = (bf16[64,2048]{1,0:T(8,128)(2,1)S(1)}, bf16[64,2048]{1,0:T(8,128)(2,1)S(1)}) custom-call(s32[24]{0:T(128)S(1)} %bitcast.21, s32[24]{0:T(128)S(1)} %bitcast.23, s32[1]{0:T(128)} %bitcast.19.live, bf16[8,24,128,128]{3,2,1,0:T(8,128)(2,1)} %more.3, bf16[8,24,128,128]{3,2,1,0:T(8,128)(2,1)} %more.3, bf16[8192,256]{1,0:T(8,128)(2,1)S(1)} %copy-done.1, ...), custom_call_target="tpu_custom_call" | custom-call | flops 134217728 | bytes 2883584 | tf_op jit(solution)/shard_map/pallas_call | solution.py:49
  6.8 4.1 %collective-permute-start = (bf16[64,2048]{1,0:T(8,128)(2,1)S(1)}, bf16[64,2048]{1,0:T(8,128)(2,1)S(1)}, u32[]{:S(2)}, u32[]{:S(2)}) collective-permute-start(bf16[64,2048]{1,0:T(8,128)(2,1)S(1)} %get-tuple-element.13.near), channel_id=1, source_target_pairs={{0,8},{4,12},{8,0},{12,4},{1,9},{5,13},{9,1},{13,5},{2,10},{6,14},... | collective-permute-start | bytes 786440 | tf_op jit(solution)/shard_map/ppermute | solution.py:149
  11.4 17.9 %collective-permute-done.far = bf16[64,2048]{1,0:T(8,128)(2,1)S(1)} collective-permute-done((bf16[64,2048]{1,0:T(8,128)(2,1)S(1)}, bf16[64,2048]{1,0:T(8,128)(2,1)S(1)}, u32[]{:S(2)}, u32[]{:S(2)}) %collective-permute-start) | collective-permute-done | bytes 262176 | tf_op jit(solution)/shard_map/ppermute | solution.py:149
  29.3 1.3 %shard_map.75 = bf16[64,2048]{1,0:T(8,128)(2,1)S(1)} custom-call(f32[8,16]{1,0:T(8,128)S(1)} %pad_maximum_fusion.2.weight, bf16[64,2048]{1,0:T(8,128)(2,1)S(1)} %get-tuple-element.13.near, bf16[64,2048]{1,0:T(8,128)(2,1)S(1)} %collective-permute-done.far), custom_call_target="tpu_custom_call" | custom-call | flops 419430400 | bytes 1048576 | tf_op jit(solution)/shard_map/pallas_call | solution.py:91
  30.7 3.5 %collective-permute-done.7.far = bf16[64,2048]{1,0:T(8,128)(2,1)S(1)} collective-permute-done((bf16[64,2048]{1,0:T(8,128)(2,1)S(1)}, bf16[64,2048]{1,0:T(8,128)(2,1)S(1)}, u32[]{:S(2)}, u32[]{:S(2)}) %collective-permute-start.7) | collective-permute-done | bytes 262176 | tf_op jit(solution)/shard_map/ppermute | solution.py:149
  34.2 1.3 %shard_map.79 = bf16[64,2048]{1,0:T(8,128)(2,1)S(1)} custom-call(f32[8,16]{1,0:T(8,128)S(1)} %pad_maximum_fusion.2.weight, bf16[64,2048]{1,0:T(8,128)(2,1)S(1)} %get-tuple-element.17.near, bf16[64,2048]{1,0:T(8,128)(2,1)S(1)} %collective-permute-done.7.far), custom_call_target="tpu_custom_call" | custom-call | flops 419430400 | bytes 1048576 | tf_op jit(solution)/shard_map/pallas_call | solution.py:91
  36.2 1.3 %shard_map.74 = f32[64,2048]{1,0:T(8,128)S(1)} custom-call(f32[8,16]{1,0:T(8,128)S(1)} %pad_maximum_fusion.1.weight, bf16[64,2048]{1,0:T(8,128)(2,1)S(1)} %get-tuple-element.13.near, bf16[64,2048]{1,0:T(8,128)(2,1)S(1)} %collective-permute-done.far), custom_call_target="tpu_custom_call" | custom-call | flops 419430400 | bytes 1048576 | tf_op jit(solution)/shard_map/pallas_call | solution.py:91
  37.4 2.4 %collective-permute-done.1 = bf16[64,2048]{1,0:T(8,128)(2,1)S(1)} collective-permute-done((bf16[64,2048]{1,0:T(8,128)(2,1)S(1)}, bf16[64,2048]{1,0:T(8,128)(2,1)S(1)}, u32[]{:S(2)}, u32[]{:S(2)}) %collective-permute-start.1) | collective-permute-done | bytes 262176 | tf_op jit(solution)/shard_map/ppermute | solution.py:149
  39.9 2.1 %collective-permute-start.3 = (bf16[64,2048]{1,0:T(8,128)(2,1)S(1)}, bf16[64,2048]{1,0:T(8,128)(2,1)S(1)}, u32[]{:S(2)}, u32[]{:S(2)}) collective-permute-start(bf16[64,2048]{1,0:T(8,128)(2,1)S(1)} %add_convert_fusion.3.refs_0_), channel_id=1, source_target_pairs={{0,2},{1,3},{2,0},{3,1},{4,6},{5,7},{6,4},{7,5},{8,10},{9,11},{10,... | collective-permute-start | bytes 786440 | tf_op jit(solution)/shard_map/ppermute | solution.py:149
  42.0 2.2 %copy-done.2 = bf16[8192,256]{1,0:T(8,128)(2,1)S(1)} copy-done((bf16[8192,256]{1,0:T(8,128)(2,1)S(1)}, bf16[8192,256]{1,0:T(8,128)(2,1)}, u32[]{:S(2)}) %copy-start.2) | copy-done | bytes 4194328
  44.2 15.3 %shard_map.76.refs_4_ = bf16[2048,2048]{1,0:T(8,128)(2,1)} custom-call(s32[24]{0:T(128)S(1)} %bitcast.22, s32[24]{0:T(128)S(1)} %bitcast.24, s32[1]{0:T(128)} %bitcast.20.live, bf16[8,24,128,128]{3,2,1,0:T(8,128)(2,1)} %more.3, bf16[8,24,128,128]{3,2,1,0:T(8,128)(2,1)} %more.3, bf16[8192,256]{1,0:T(8,128)(2,1)S(1)} %copy-done.2, ...), custom_call_target="tpu_custom_call" | custom-call | flops 2147483648 | bytes 14680064 | tf_op jit(solution)/shard_map/pallas_call | solution.py:49
  59.5 1.3 %shard_map.78 = f32[64,2048]{1,0:T(8,128)S(1)} custom-call(f32[8,16]{1,0:T(8,128)S(1)} %pad_maximum_fusion.1.weight, bf16[64,2048]{1,0:T(8,128)(2,1)S(1)} %get-tuple-element.17.near, bf16[64,2048]{1,0:T(8,128)(2,1)S(1)} %collective-permute-done.7.far), custom_call_target="tpu_custom_call" | custom-call | flops 419430400 | bytes 1048576 | tf_op jit(solution)/shard_map/pallas_call | solution.py:91
  60.7 1.3 %collective-permute-start.2 = (bf16[64,2048]{1,0:T(8,128)(2,1)S(1)}, bf16[64,2048]{1,0:T(8,128)(2,1)S(1)}, u32[]{:S(2)}, u32[]{:S(2)}) collective-permute-start(bf16[64,2048]{1,0:T(8,128)(2,1)S(1)} %add_convert_fusion.3.refs_0_), channel_id=1, source_target_pairs={{0,1},{1,0},{2,3},{3,2},{4,5},{5,4},{6,7},{7,6},{8,9},{9,8},{10,11... | collective-permute-start | bytes 786440 | tf_op jit(solution)/shard_map/ppermute | solution.py:149
  63.6 6.3 %shard_map.77 = (bf16[128,2048]{1,0:T(8,128)(2,1)S(1)}, f32[64,2048]{1,0:T(8,128)S(1)}, f32[64,2048]{1,0:T(8,128)S(1)}) custom-call(s32[4]{0:T(128)S(1)} %gather_fusion, bf16[64,2048]{1,0:T(8,128)(2,1)S(1)} %add_convert_fusion.3.refs_0_, bf16[64,2048]{1,0:T(8,128)(2,1)S(1)} %collective-permute-done.2.refs_1_, ...), custom_call_target="tpu_custom_call" | custom-call | flops 2147483648 | bytes 9437184 | tf_op jit(solution)/shard_map/pallas_call | solution.py:123
  71.6 0.9 collective-permute-done.11.refs_3_
  72.5 6.3 %shard_map.80 = (bf16[128,2048]{1,0:T(8,128)(2,1)S(1)}, f32[64,2048]{1,0:T(8,128)S(1)}, f32[64,2048]{1,0:T(8,128)S(1)}) custom-call(s32[4]{0:T(128)S(1)} %gather_fusion, bf16[64,2048]{1,0:T(8,128)(2,1)S(1)} %add_convert_fusion.1.refs_0_, bf16[64,2048]{1,0:T(8,128)(2,1)S(1)} %collective-permute-done.9.refs_1_, ...), custom_call_target="tpu_custom_call" | custom-call | flops 2147483648 | bytes 9437184 | tf_op jit(solution)/shard_map/pallas_call | solution.py:123
  78.8 1.5 %collective-permute-start.12 = (bf16[128,2048]{1,0:T(8,128)(2,1)S(1)}, bf16[128,2048]{1,0:T(8,128)(2,1)S(1)}, u32[]{:S(2)}, u32[]{:S(2)}) collective-permute-start(bf16[128,2048]{1,0:T(8,128)(2,1)S(1)} %get-tuple-element.19), channel_id=1, source_target_pairs={{0,4},{4,0},{8,12},{12,8},{1,5},{5,1},{9,13},{13,9},{2,6},{6,2},{1... | collective-permute-start | bytes 1572872 | tf_op jit(solution)/shard_map/ppermute | solution.py:149
  80.3 4.5 %collective-permute-done.5 = bf16[128,2048]{1,0:T(8,128)(2,1)S(1)} collective-permute-done((bf16[128,2048]{1,0:T(8,128)(2,1)S(1)}, bf16[128,2048]{1,0:T(8,128)(2,1)S(1)}, u32[]{:S(2)}, u32[]{:S(2)}) %collective-permute-start.5) | collective-permute-done | bytes 524320 | tf_op jit(solution)/shard_map/ppermute | solution.py:149
  84.8 1.3 %collective-permute-start.6 = (bf16[64,2048]{1,0:T(8,128)(2,1)S(1)}, bf16[64,2048]{1,0:T(8,128)(2,1)S(1)}, u32[]{:S(2)}, u32[]{:S(2)}) collective-permute-start(bf16[64,2048]{1,0:T(8,128)(2,1)S(1)} %add_convert_fusion.2), channel_id=1, source_target_pairs={{0,8},{4,12},{8,0},{12,4},{1,9},{5,13},{9,1},{13,5},{2,10},{6,14},... | collective-permute-start | bytes 786440 | tf_op jit(solution)/shard_map/ppermute | solution.py:149
  86.1 14.9 %collective-permute-done.12 = bf16[128,2048]{1,0:T(8,128)(2,1)S(1)} collective-permute-done((bf16[128,2048]{1,0:T(8,128)(2,1)S(1)}, bf16[128,2048]{1,0:T(8,128)(2,1)S(1)}, u32[]{:S(2)}, u32[]{:S(2)}) %collective-permute-start.12) | collective-permute-done | bytes 524320 | tf_op jit(solution)/shard_map/ppermute | solution.py:149
  101.1 0.7 collective-permute-start.13
  101.9 13.2 %collective-permute-done.13 = bf16[64,2048]{1,0:T(8,128)(2,1)S(1)} collective-permute-done((bf16[64,2048]{1,0:T(8,128)(2,1)S(1)}, bf16[64,2048]{1,0:T(8,128)(2,1)S(1)}, u32[]{:S(2)}, u32[]{:S(2)}) %collective-permute-start.13) | collective-permute-done | bytes 262176 | tf_op jit(solution)/shard_map/ppermute | solution.py:149
  115.2 1.1 pad_maximum_fusion
  (43 shorter events, 6.1 us)
Async XLA Ops:
  0.0 11.0 %copy-start = (bf16[32,32]{1,0:T(8,128)(2,1)S(1)}, bf16[32,32]{1,0:T(8,128)(2,1)}, u32[]{:S(2)}) copy-start(bf16[32,32]{1,0:T(8,128)(2,1)} %param.12) | copy-start | bytes 6148
  0.7 2.2 %copy-start.1 = (bf16[8192,256]{1,0:T(8,128)(2,1)S(1)}, bf16[8192,256]{1,0:T(8,128)(2,1)}, u32[]{:S(2)}) copy-start(bf16[8192,256]{1,0:T(8,128)(2,1)} %rest_7_.3) | copy-start | bytes 12582916
  2.9 0.7 copy-start.3
  3.5 0.7 copy-start.5
  4.2 37.8 %copy-start.4 = (s32[1,24]{1,0:T(1,128)S(1)}, s32[1,24]{1,0:T(1,128)}, u32[]{:S(2)}) copy-start(s32[1,24]{1,0:T(1,128)} %param.8) | copy-start | bytes 292
  4.2 37.8 %copy-start.6 = (s32[1,24]{1,0:T(1,128)S(1)}, s32[1,24]{1,0:T(1,128)}, u32[]{:S(2)}) copy-start(s32[1,24]{1,0:T(1,128)} %param.9) | copy-start | bytes 292
  6.8 22.5 %collective-permute-start = (bf16[64,2048]{1,0:T(8,128)(2,1)S(1)}, bf16[64,2048]{1,0:T(8,128)(2,1)S(1)}, u32[]{:S(2)}, u32[]{:S(2)}) collective-permute-start(bf16[64,2048]{1,0:T(8,128)(2,1)S(1)} %get-tuple-element.13.near), channel_id=1, source_target_pairs={{0,8},{4,12},{8,0},{12,4},{1,9},{5,13},{9,1},{13,5},{2,10},{6,14},... | collective-permute-start | bytes 786440 | tf_op jit(solution)/shard_map/ppermute | solution.py:149
  10.9 23.3 %collective-permute-start.7 = (bf16[64,2048]{1,0:T(8,128)(2,1)S(1)}, bf16[64,2048]{1,0:T(8,128)(2,1)S(1)}, u32[]{:S(2)}, u32[]{:S(2)}) collective-permute-start(bf16[64,2048]{1,0:T(8,128)(2,1)S(1)} %get-tuple-element.17.near), channel_id=1, source_target_pairs={{0,8},{4,12},{8,0},{12,4},{1,9},{5,13},{9,1},{13,5},{2,10},{6,14},... | collective-permute-start | bytes 786440 | tf_op jit(solution)/shard_map/ppermute | solution.py:149
  30.6 9.2 %collective-permute-start.1 = (bf16[64,2048]{1,0:T(8,128)(2,1)S(1)}, bf16[64,2048]{1,0:T(8,128)(2,1)S(1)}, u32[]{:S(2)}, u32[]{:S(2)}) collective-permute-start(bf16[64,2048]{1,0:T(8,128)(2,1)S(1)} %shard_map.75), channel_id=1, source_target_pairs={{0,4},{4,0},{8,12},{12,8},{1,5},{5,1},{9,13},{13,9},{2,6},{6,2},{1... | collective-permute-start | bytes 786440 | tf_op jit(solution)/shard_map/ppermute | solution.py:149
  35.5 26.7 %collective-permute-start.8 = (bf16[64,2048]{1,0:T(8,128)(2,1)S(1)}, bf16[64,2048]{1,0:T(8,128)(2,1)S(1)}, u32[]{:S(2)}, u32[]{:S(2)}) collective-permute-start(bf16[64,2048]{1,0:T(8,128)(2,1)S(1)} %shard_map.79), channel_id=1, source_target_pairs={{0,4},{4,0},{8,12},{12,8},{1,5},{5,1},{9,13},{13,9},{2,6},{6,2},{1... | collective-permute-start | bytes 786440 | tf_op jit(solution)/shard_map/ppermute | solution.py:149
  39.9 22.2 %collective-permute-start.3 = (bf16[64,2048]{1,0:T(8,128)(2,1)S(1)}, bf16[64,2048]{1,0:T(8,128)(2,1)S(1)}, u32[]{:S(2)}, u32[]{:S(2)}) collective-permute-start(bf16[64,2048]{1,0:T(8,128)(2,1)S(1)} %add_convert_fusion.3.refs_0_), channel_id=1, source_target_pairs={{0,2},{1,3},{2,0},{3,1},{4,6},{5,7},{6,4},{7,5},{8,10},{9,11},{10,... | collective-permute-start | bytes 786440 | tf_op jit(solution)/shard_map/ppermute | solution.py:149
  42.0 2.2 %copy-start.2 = (bf16[8192,256]{1,0:T(8,128)(2,1)S(1)}, bf16[8192,256]{1,0:T(8,128)(2,1)}, u32[]{:S(2)}) copy-start(bf16[8192,256]{1,0:T(8,128)(2,1)} %rest_7_.3) | copy-start | bytes 12582916
  44.2 18.6 %copy-start.7 = (s32[4]{0:T(128)S(1)}, s32[4]{0:T(128)}, u32[]{:S(2)}) copy-start(s32[4]{0:T(128)} %constant.19.clone) | copy-start | bytes 52
  60.7 2.6 %collective-permute-start.2 = (bf16[64,2048]{1,0:T(8,128)(2,1)S(1)}, bf16[64,2048]{1,0:T(8,128)(2,1)S(1)}, u32[]{:S(2)}, u32[]{:S(2)}) collective-permute-start(bf16[64,2048]{1,0:T(8,128)(2,1)S(1)} %add_convert_fusion.3.refs_0_), channel_id=1, source_target_pairs={{0,1},{1,0},{2,3},{3,2},{4,5},{5,4},{6,7},{7,6},{8,9},{9,8},{10,11... | collective-permute-start | bytes 786440 | tf_op jit(solution)/shard_map/ppermute | solution.py:149
  62.1 1.5 %collective-permute-start.4 = (bf16[64,2048]{1,0:T(8,128)(2,1)S(1)}, bf16[64,2048]{1,0:T(8,128)(2,1)S(1)}, u32[]{:S(2)}, u32[]{:S(2)}) collective-permute-start(bf16[64,2048]{1,0:T(8,128)(2,1)S(1)} %collective-permute-done.3.refs_2_), channel_id=1, source_target_pairs={{0,1},{1,0},{2,3},{3,2},{4,5},{5,4},{6,7},{7,6},{8,9},{9,8},{10,11... | collective-permute-start | bytes 786440 | tf_op jit(solution)/shard_map/ppermute | solution.py:149
  62.2 8.7 %collective-permute-start.10 = (bf16[64,2048]{1,0:T(8,128)(2,1)S(1)}, bf16[64,2048]{1,0:T(8,128)(2,1)S(1)}, u32[]{:S(2)}, u32[]{:S(2)}) collective-permute-start(bf16[64,2048]{1,0:T(8,128)(2,1)S(1)} %add_convert_fusion.1.refs_0_), channel_id=1, source_target_pairs={{0,2},{1,3},{2,0},{3,1},{4,6},{5,7},{6,4},{7,5},{8,10},{9,11},{10,... | collective-permute-start | bytes 786440 | tf_op jit(solution)/shard_map/ppermute | solution.py:149
  69.9 14.8 %collective-permute-start.5 = (bf16[128,2048]{1,0:T(8,128)(2,1)S(1)}, bf16[128,2048]{1,0:T(8,128)(2,1)S(1)}, u32[]{:S(2)}, u32[]{:S(2)}) collective-permute-start(bf16[128,2048]{1,0:T(8,128)(2,1)S(1)} %get-tuple-element.15), channel_id=1, source_target_pairs={{0,4},{4,0},{8,12},{12,8},{1,5},{5,1},{9,13},{13,9},{2,6},{6,2},{1... | collective-permute-start | bytes 1572872 | tf_op jit(solution)/shard_map/ppermute | solution.py:149
  70.0 1.6 %collective-permute-start.9 = (bf16[64,2048]{1,0:T(8,128)(2,1)S(1)}, bf16[64,2048]{1,0:T(8,128)(2,1)S(1)}, u32[]{:S(2)}, u32[]{:S(2)}) collective-permute-start(bf16[64,2048]{1,0:T(8,128)(2,1)S(1)} %add_convert_fusion.1.refs_0_), channel_id=1, source_target_pairs={{0,1},{1,0},{2,3},{3,2},{4,5},{5,4},{6,7},{7,6},{8,9},{9,8},{10,11... | collective-permute-start | bytes 786440 | tf_op jit(solution)/shard_map/ppermute | solution.py:149
  70.9 1.5 %collective-permute-start.11 = (bf16[64,2048]{1,0:T(8,128)(2,1)S(1)}, bf16[64,2048]{1,0:T(8,128)(2,1)S(1)}, u32[]{:S(2)}, u32[]{:S(2)}) collective-permute-start(bf16[64,2048]{1,0:T(8,128)(2,1)S(1)} %collective-permute-done.10.refs_2_), channel_id=1, source_target_pairs={{0,1},{1,0},{2,3},{3,2},{4,5},{5,4},{6,7},{7,6},{8,9},{9,8},{10,11... | collective-permute-start | bytes 786440 | tf_op jit(solution)/shard_map/ppermute | solution.py:149
  78.8 22.2 %collective-permute-start.12 = (bf16[128,2048]{1,0:T(8,128)(2,1)S(1)}, bf16[128,2048]{1,0:T(8,128)(2,1)S(1)}, u32[]{:S(2)}, u32[]{:S(2)}) collective-permute-start(bf16[128,2048]{1,0:T(8,128)(2,1)S(1)} %get-tuple-element.19), channel_id=1, source_target_pairs={{0,4},{4,0},{8,12},{12,8},{1,5},{5,1},{9,13},{13,9},{2,6},{6,2},{1... | collective-permute-start | bytes 1572872 | tf_op jit(solution)/shard_map/ppermute | solution.py:149
  84.8 17.0 %collective-permute-start.6 = (bf16[64,2048]{1,0:T(8,128)(2,1)S(1)}, bf16[64,2048]{1,0:T(8,128)(2,1)S(1)}, u32[]{:S(2)}, u32[]{:S(2)}) collective-permute-start(bf16[64,2048]{1,0:T(8,128)(2,1)S(1)} %add_convert_fusion.2), channel_id=1, source_target_pairs={{0,8},{4,12},{8,0},{12,4},{1,9},{5,13},{9,1},{13,5},{2,10},{6,14},... | collective-permute-start | bytes 786440 | tf_op jit(solution)/shard_map/ppermute | solution.py:149
  101.1 14.0 %collective-permute-start.13 = (bf16[64,2048]{1,0:T(8,128)(2,1)S(1)}, bf16[64,2048]{1,0:T(8,128)(2,1)S(1)}, u32[]{:S(2)}, u32[]{:S(2)}) collective-permute-start(bf16[64,2048]{1,0:T(8,128)(2,1)S(1)} %add_convert_fusion), channel_id=1, source_target_pairs={{0,8},{4,12},{8,0},{12,4},{1,9},{5,13},{9,1},{13,5},{2,10},{6,14},... | collective-permute-start | bytes 786440 | tf_op jit(solution)/shard_map/ppermute | solution.py:149

commit v2 on v0

v2 whole, which is shorter than its diff:
```python
import functools

import jax
import jax.numpy as jnp
from jax import lax
from jax.experimental import pallas as pl
from jax.experimental.pallas import tpu as pltpu
from jax.sharding import PartitionSpec as P

KR = 128
HALVES = 2
LIMIT = 8 * 1024 * 1024
WHOLE = 60 * 1024 * 1024
F32 = jnp.float32
BF16 = jnp.bfloat16


def add_slot(acc, tile, orb, fresh):
    aux_dev, width, _ = tile.shape
    term = jnp.dot(tile.reshape(aux_dev * width, width), orb, preferred_element_type=F32)
    acc[...] = term if fresh else acc[...] + term


def store_block(acc, outs, row, aux_dev):
    occ = acc.shape[1]
    width = acc.shape[0] // aux_dev
    part = width // len(outs)
    for k, out in enumerate(outs):
        for q in range(aux_dev):
            first = q * width + k * part
            out[pl.ds(row, part), q * occ:(q + 1) * occ] = acc[first:first + part, :].astype(BF16)


def window_body(blocks, outs, rows, cols, live, tiles, orbitals, *rest):
    out_refs, tile, orb, acc, tile_sems, orb_sems = rest[:outs], *rest[outs:]
    aux_dev, slots, width, _ = tiles.shape

    def copies(k, slot):
        row = pl.multiple_of(cols[0, slot] * width, width)
        return (pltpu.make_async_copy(tiles.at[:, slot], tile.at[k], tile_sems.at[k]),
                pltpu.make_async_copy(orbitals.at[pl.ds(row, width)], orb.at[k], orb_sems.at[k]))

    def wanted(slot):
        return (rows[0, slot] == 0) & (slot < live[0, 0])

    for copy in copies(0, 0):
        copy.start()
    for slot in range(blocks, slots):
        @pl.when(wanted(slot))
        def _():
            for copy in copies(slot - blocks + 1, slot):
                copy.start()
    for copy in copies(0, 0):
        copy.wait()
    add_slot(acc, tile[0], orb[0], True)
    for slot in range(blocks, slots):
        @pl.when(wanted(slot))
        def _():
            k = slot - blocks + 1
            for copy in copies(k, slot):
                copy.wait()
            add_slot(acc, tile[k], orb[k], False)
    store_block(acc, out_refs, 0, aux_dev)


def window_rows(tiles, rows, cols, live, orbitals, outs):
    aux_dev, slots, width, _ = tiles.shape
    basis, occ = orbitals.shape
    blocks = basis // (width * lax.axis_size("row"))
    held = slots - blocks + 1
    smem, hbm = pl.BlockSpec(memory_space=pltpu.SMEM), pl.BlockSpec(memory_space=pltpu.HBM)
    return pl.pallas_call(
        functools.partial(window_body, blocks, outs),
        in_specs=[smem] * 3 + [hbm] * 2,
        out_specs=[pl.BlockSpec(memory_space=pltpu.VMEM)] * outs,
        out_shape=[jax.ShapeDtypeStruct((width // outs, aux_dev * occ), BF16)] * outs,
        scratch_shapes=[
            pltpu.VMEM((held, aux_dev, width, width), BF16),
            pltpu.VMEM((held, width, occ), BF16),
            pltpu.VMEM((aux_dev * width, occ), F32),
            pltpu.SemaphoreType.DMA((held,)),
            pltpu.SemaphoreType.DMA((held,)),
        ],
        compiler_params=pltpu.CompilerParams(vmem_limit_bytes=WHOLE),
        cost_estimate=pl.CostEstimate(
            flops=4 * aux_dev * width * width * occ, bytes_accessed=4 * aux_dev * width * width,
            transcendentals=0),
    )(rows, cols, live, tiles, orbitals)


def half_body(blocks, rows, cols, live, tiles, orbitals, weights, out, same, acc):
    same[...] = weights[...]
    aux_dev, slots, width, _ = tiles.shape

    def columns(slot):
        return orbitals[pl.ds(pl.multiple_of(cols[0, slot] * width, width), width), :]

    def block(b, carry):
        add_slot(acc, tiles[:, b], columns(b), True)

        def extra(slot, inner):
            @pl.when(rows[0, slot] == b)
            def _():
                add_slot(acc, tiles[:, slot], columns(slot), False)
            return inner

        lax.fori_loop(blocks, jnp.minimum(live[0, 0], slots), extra, 0)
        store_block(acc, [out], pl.multiple_of(b * width, width), aux_dev)
        return carry

    lax.fori_loop(0, blocks, block, 0)


def half_rows(tiles, rows, cols, live, orbitals, weights):
    aux_dev, slots, width, _ = tiles.shape
    basis, occ = orbitals.shape
    blocks = basis // (width * lax.axis_size("row"))
    wide = aux_dev * occ
    smem, vmem = pl.BlockSpec(memory_space=pltpu.SMEM), pl.BlockSpec(memory_space=pltpu.VMEM)
    return pl.pallas_call(
        functools.partial(half_body, blocks),
        in_specs=[smem] * 3 + [vmem] * 3,
        out_specs=[vmem] * 2,
        out_shape=[
            jax.ShapeDtypeStruct((blocks * width, wide), BF16),
            jax.ShapeDtypeStruct(weights.shape, weights.dtype),
        ],
        scratch_shapes=[pltpu.VMEM((aux_dev * width, occ), F32)],
        compiler_params=pltpu.CompilerParams(vmem_limit_bytes=LIMIT),
        cost_estimate=pl.CostEstimate(
            flops=4 * slots * aux_dev * width * width * occ,
            bytes_accessed=2 * (slots * aux_dev * width * width + basis * occ + blocks * width * wide),
            transcendentals=0),
    )(rows, cols, live, tiles, orbitals, weights)


def mix_body(occ, which, weight, near, far, out):
    outs_q = out.shape[1] // occ
    ins_q = near.shape[1] // occ
    step = 16

    def chunk(c, carry):
        span = pl.ds(pl.multiple_of(c * step, step), step)
        sums = [None] * outs_q
        for k in range(2 * ins_q):
            ref, q = (near, k) if k < ins_q else (far, k - ins_q)
            x = ref[span, q * occ:(q + 1) * occ].astype(F32)
            for p in range(outs_q):
                term = x * weight[which, p, k]
                sums[p] = term if sums[p] is None else sums[p] + term
        for p in range(outs_q):
            out[span, p * occ:(p + 1) * occ] = sums[p].astype(out.dtype)
        return carry

    lax.fori_loop(0, near.shape[0] // step, chunk, 0)


def mix(weight, which, near, far, occ, dtype):
    rows, wide = near.shape
    return pl.pallas_call(
        functools.partial(mix_body, occ, which),
        in_specs=[pl.BlockSpec(memory_space=pltpu.SMEM)] + [pl.BlockSpec(memory_space=pltpu.VMEM)] * 2,
        out_specs=pl.BlockSpec(memory_space=pltpu.VMEM),
        out_shape=jax.ShapeDtypeStruct((rows, wide), dtype),
        compiler_params=pltpu.CompilerParams(vmem_limit_bytes=LIMIT),
        cost_estimate=pl.CostEstimate(
            flops=2 * rows * wide * weight.shape[2], bytes_accessed=8 * rows * wide, transcendentals=0),
    )(weight, near, far)


def product_body(flag, even, odd, right, send, keep, left):
    rows, count = even.shape[0], right.shape[0]
    step = 512
    for k, piece in ((0, even), (1, odd)):
        place = jnp.where(flag[0] == k, rows, 0)
        left[pl.ds(pl.multiple_of(place, rows), rows), :] = piece[...]

    for n in range(count // step):
        product = lax.dot_general(
            left[...], right[n * step:(n + 1) * step, :], (((1,), (1,)), ((), ())),
            preferred_element_type=F32)
        send[:, n * step:(n + 1) * step] = product[:rows].astype(BF16)
        keep[:, n * step:(n + 1) * step] = product[rows:]


def product_rows(flag, even, odd, right):
    rows, wide = even.shape
    count = right.shape[0]
    vmem = pl.BlockSpec(memory_space=pltpu.VMEM)
    return pl.pallas_call(
        product_body,
        in_specs=[pl.BlockSpec(memory_space=pltpu.SMEM)] + [vmem] * 3,
        out_specs=[vmem] * 2,
        scratch_shapes=[pltpu.VMEM((2 * rows, wide), BF16)],
        out_shape=[
            jax.ShapeDtypeStruct((rows, count), BF16),
            jax.ShapeDtypeStruct((rows, count), F32),
        ],
        compiler_params=pltpu.CompilerParams(vmem_limit_bytes=LIMIT),
        cost_estimate=pl.CostEstimate(
            flops=4 * rows * wide * count, bytes_accessed=2 * wide * (count + 2 * rows), transcendentals=0),
    )(flag, even, odd, right)


def swap(x, axis, distance):
    size = lax.axis_size(axis)
    return lax.ppermute(x, axis, [(i, i ^ distance) for i in range(size)])


def forward(x, late):
    pairs = []
    for z in range(4):
        for r in range(4):
            if ((z ^ r) & 2 == 0) == late:
                pairs.append((z * 4 + r, (z ^ 2) * 4 + r))
    return lax.ppermute(x, ("aux", "row"), pairs)


def four_by_four(args, squared):
    aux_dev, occ = args[0].shape[0], args[-1].shape[1]
    z, r = lax.axis_index("aux"), lax.axis_index("row")
    table = squared.reshape(4, aux_dev, 4, aux_dev)
    pick = lambda p, q: table[p, :, q, :]
    weights = jnp.stack([jnp.concatenate([pick(p, z), pick(p, z ^ 2)], axis=1) for p in (z ^ 1, z)])
    window = window_rows(*args, HALVES)
    flag = jnp.reshape((r ^ z) & 1, (1,))
    first_own = ((r ^ z) & 2) == 0
    fars = [swap(x, "aux", 2) for x in window]
    right, weights = half_rows(*args, weights)
    pieces = []
    for x, far in zip(window, fars):
        message = swap(mix(weights, 0, x, far, occ, BF16), "aux", 1)
        mine = mix(weights, 1, x, far, occ, F32)
        g0 = (mine + message.astype(F32)).astype(BF16)
        g1 = swap(g0, "row", 1)
        g2 = swap(g0, "row", 2)
        g3 = swap(g2, "row", 1)
        pieces.append(((g0, g1), (g2, g3)))
    sums = [[], []]
    for late in (0, 1):
        for piece in pieces:
            send, keep = product_rows(flag, *piece[late], right)
            came = swap(send, "aux", 1)
            total = keep + came.astype(F32)
            passed = forward(total.astype(BF16), late == 1)
            sums[late].append((total, passed))
    results = [
        jnp.where(first_own, early, late) + passed_early.astype(F32) + passed_late.astype(F32)
        for (early, passed_early), (late, passed_late) in zip(*sums)
    ]
    return jnp.concatenate(results, axis=0)


def any_mesh(args, squared):
    aux_dev, occ = args[0].shape[0], args[-1].shape[1]
    window, = window_rows(*args, 1)
    right, squared = half_rows(*args, squared)
    rows = window.shape[0]
    aux = lax.axis_size("aux")
    gathered = lax.all_gather(window, "aux", axis=0, tiled=True).reshape(aux, rows, aux_dev, occ)
    own = lax.dynamic_slice_in_dim(squared, lax.axis_index("aux") * aux_dev, aux_dev, 0)
    own = own.reshape(aux_dev, aux, aux_dev)
    mixed = jnp.einsum("paq,amqi->mpi", own, gathered.astype(F32), precision=lax.Precision.HIGHEST)
    left = lax.all_gather(mixed.astype(BF16).reshape(rows, -1), "row", axis=0, tiled=True)
    product = lax.dot_general(left, right, (((1,), (1,)), ((), ())), preferred_element_type=F32)
    return lax.psum_scatter(product, "aux", scatter_dimension=0, tiled=True)


def shards(tensor_tiles, pair_rows, pair_cols, live_count, orbitals, metric):
    squared = jnp.dot(metric.T, metric, preferred_element_type=F32)
    args = (tensor_tiles, pair_rows, pair_cols, live_count, orbitals)
    if lax.axis_size("aux") == 4 and lax.axis_size("row") == 4:
        return four_by_four(args, squared)
    return any_mesh(args, squared)


def solution(mesh):
    return jax.shard_map(
        shards,
        mesh=mesh,
        in_specs=(
            P(("groups", "aux"), "row", None, None),
            P(("groups", "aux"), "row"),
            P(("groups", "aux"), "row"),
            P(("groups", "aux"), "row"),
            P(None, "groups"),
            P(),
        ),
        out_specs=P(("groups", "aux"), "row"),
        check_vma=False,
    )
```

time: 486 us -> 104 us (0.21)
  the two profiles are of different devices: /device:TPU:0 before, /device:TPU:6 now
where the time goes in v2:
time: 104 us
  waiting for transfers between devices  38.7 us (37%)
  Pallas kernels  26.9 us (26%)
  starting transfers between devices  19.9 us (19%)
  local copies, waits for them, and re-layouts  15.1 us (15%)
  other arithmetic  1.82 us (2%)
    ppermute x14, waiting for transfers between devices, swap(): return lax.ppermute(x, axis, [(i, i ^ distance) for i in range(size)])  24 us
    unnamed x22, local copies, waits for them, and re-layouts  15 us
    ppermute x4, waiting for transfers between devices, forward(): return lax.ppermute(x, ('aux', 'row'), pairs)  14.7 us
    pallas_call x4, Pallas kernels, product_rows(): pl.pallas_call(product_body, in_specs=[pl.BlockSpec(memory_space=pltpu.SM...  11.6 us
    ppermute x14, starting transfers between devices, swap(): return lax.ppermute(x, axis, [(i, i ^ distance) for i in range(size)])  11.1 us
    ppermute x4, starting transfers between devices, forward(): return lax.ppermute(x, ('aux', 'row'), pairs)  8.81 us
    pallas_call x1, Pallas kernels, half_rows(): pl.pallas_call(functools.partial(half_body, blocks), in_specs=[smem] * 3...  6.92 us
    pallas_call x4, Pallas kernels, mix(): pl.pallas_call(functools.partial(mix_body, occ, which), in_specs=[pl.Bloc...  5.36 us
  transfers between devices with their start and end apart: 18, of which 8 were waited for; matrix products, arithmetic and copies ran while one was open for 1% of the time, Pallas kernels for 23%

profile of v2, /device:TPU:6, one launch (start us, length us, event | category | flops | bytes accessed | tf_op | source)
XLA Modules:
  0.0 103.6 jit_solution(14619277858208228557)
XLA Ops:
  0.7 3.0 %shard_map.65 = (bf16[64,2048]{1,0:T(8,128)(2,1)}, bf16[64,2048]{1,0:T(8,128)(2,1)}) custom-call(s32[1,24]{1,0:T(1,128)} %rows.3, s32[1,24]{1,0:T(1,128)} %cols.3, s32[1,1]{1,0:T(1,128)S(6)} %copy.15.live, bf16[8,24,128,128]{3,2,1,0:T(8,128)(2,1)} %tiles.3, bf16[8192,256]{1,0:T(8,128)(2,1)} %orbitals.3), custom_call_target="tpu_custom_call" | custom-call | flops 134217728 | bytes 524288 | tf_op jit(solution)/shard_map/pallas_call | solution.py:72
  3.7 2.6 %collective-permute-start = (bf16[64,2048]{1,0:T(8,128)(2,1)}, bf16[64,2048]{1,0:T(8,128)(2,1)S(1)}, u32[]{:S(2)}, u32[]{:S(2)}) collective-permute-start(bf16[64,2048]{1,0:T(8,128)(2,1)} %get-tuple-element.18.near), channel_id=1, source_target_pairs={{0,8},{4,12},{8,0},{12,4},{1,9},{5,13},{9,1},{13,5},{2,10},{6,14},... | collective-permute-start | bytes 786440 | tf_op jit(solution)/shard_map/ppermute | solution.py:207
  7.1 2.8 %copy-done.5 = bf16[8,24,128,128]{3,2,1,0:T(8,128)(2,1)S(1)} copy-done((bf16[8,24,128,128]{3,2,1,0:T(8,128)(2,1)S(1)}, bf16[8,24,128,128]{3,2,1,0:T(8,128)(2,1)}, u32[]{:S(2)}) %copy-start.5) | copy-done | bytes 6291480
  9.9 2.2 %copy-done.6 = bf16[8192,256]{1,0:T(8,128)(2,1)S(1)} copy-done((bf16[8192,256]{1,0:T(8,128)(2,1)S(1)}, bf16[8192,256]{1,0:T(8,128)(2,1)}, u32[]{:S(2)}) %copy-start.6) | copy-done | bytes 4194328
  12.1 6.9 %shard_map.64 = (bf16[2048,2048]{1,0:T(8,128)(2,1)S(1)}, f32[2,8,16]{2,1,0:T(8,128)S(1)}) custom-call(s32[1,24]{1,0:T(1,128)S(1)} %copy-done.9, s32[1,24]{1,0:T(1,128)S(1)} %copy-done.10, s32[1,1]{1,0:T(1,128)S(6)} %copy.15.live, bf16[8,24,128,128]{3,2,1,0:T(8,128)(2,1)S(1)} %copy-done.5, bf16[8192,256]{1,0:T(8,128)(2,1)S(1)} %copy-done.6, ...), custom_call_target="tpu_custom_call" | custom-call | flops 3221225472 | bytes 18874368 | tf_op jit(solution)/shard_map/pallas_call | solution.py:120
  19.0 3.3 %copy-done.1 = bf16[2048,2048]{1,0:T(8,128)(2,1)} copy-done((bf16[2048,2048]{1,0:T(8,128)(2,1)}, bf16[2048,2048]{1,0:T(8,128)(2,1)S(1)}, u32[]{:S(2)}) %copy-start.1) | copy-done | bytes 8388632
  22.3 3.0 %collective-permute-done.far = bf16[64,2048]{1,0:T(8,128)(2,1)S(1)} collective-permute-done((bf16[64,2048]{1,0:T(8,128)(2,1)}, bf16[64,2048]{1,0:T(8,128)(2,1)S(1)}, u32[]{:S(2)}, u32[]{:S(2)}) %collective-permute-start) | collective-permute-done | bytes 262176 | tf_op jit(solution)/shard_map/ppermute | solution.py:207
  26.7 3.4 %collective-permute-done.9.far = bf16[64,2048]{1,0:T(8,128)(2,1)S(1)} collective-permute-done((bf16[64,2048]{1,0:T(8,128)(2,1)}, bf16[64,2048]{1,0:T(8,128)(2,1)S(1)}, u32[]{:S(2)}, u32[]{:S(2)}) %collective-permute-start.9) | collective-permute-done | bytes 262176 | tf_op jit(solution)/shard_map/ppermute | solution.py:207
  36.0 5.3 %collective-permute-done.10 = bf16[64,2048]{1,0:T(8,128)(2,1)S(1)} collective-permute-done((bf16[64,2048]{1,0:T(8,128)(2,1)S(1)}, bf16[64,2048]{1,0:T(8,128)(2,1)S(1)}, u32[]{:S(2)}, u32[]{:S(2)}) %collective-permute-start.10) | collective-permute-done | bytes 262176 | tf_op jit(solution)/shard_map/ppermute | solution.py:207
  41.7 1.8 %collective-permute-start.13 = (bf16[64,2048]{1,0:T(8,128)(2,1)S(1)}, bf16[64,2048]{1,0:T(8,128)(2,1)S(1)}, u32[]{:S(2)}, u32[]{:S(2)}) collective-permute-start(bf16[64,2048]{1,0:T(8,128)(2,1)S(1)} %add_convert_fusion.even), channel_id=1, source_target_pairs={{0,2},{1,3},{2,0},{3,1},{4,6},{5,7},{6,4},{7,5},{8,10},{9,11},{10,... | collective-permute-start | bytes 786440 | tf_op jit(solution)/shard_map/ppermute | solution.py:207
  43.5 3.4 %copy-done.2 = bf16[2048,2048]{1,0:T(8,128)(2,1)S(1)} copy-done((bf16[2048,2048]{1,0:T(8,128)(2,1)S(1)}, bf16[2048,2048]{1,0:T(8,128)(2,1)}, u32[]{:S(2)}) %copy-start.2) | copy-done | bytes 8388632
  46.9 2.9 %shard_map.68 = (bf16[64,2048]{1,0:T(8,128)(2,1)S(1)}, f32[64,2048]{1,0:T(8,128)S(1)}) custom-call(s32[1]{0:T(128)} %bitcast.flag, bf16[64,2048]{1,0:T(8,128)(2,1)S(1)} %add_convert_fusion.1.even, bf16[64,2048]{1,0:T(8,128)(2,1)S(1)} %collective-permute-done.2.odd, bf16[2048,2048]{1,0:T(8,128)(2,1)S(1)} %copy-done.2), custom_call_target="tpu_custom_call" | custom-call | flops 1073741824 | bytes 8912896 | tf_op jit(solution)/shard_map/pallas_call | solution.py:190
  49.9 3.4 %copy-done.3 = bf16[2048,2048]{1,0:T(8,128)(2,1)S(1)} copy-done((bf16[2048,2048]{1,0:T(8,128)(2,1)S(1)}, bf16[2048,2048]{1,0:T(8,128)(2,1)}, u32[]{:S(2)}) %copy-start.3) | copy-done | bytes 8388632
  53.2 2.9 %shard_map.72 = (bf16[64,2048]{1,0:T(8,128)(2,1)S(1)}, f32[64,2048]{1,0:T(8,128)S(1)}) custom-call(s32[1]{0:T(128)} %bitcast.flag, bf16[64,2048]{1,0:T(8,128)(2,1)S(1)} %add_convert_fusion.even, bf16[64,2048]{1,0:T(8,128)(2,1)S(1)} %collective-permute-done.11.odd, bf16[2048,2048]{1,0:T(8,128)(2,1)S(1)} %copy-done.3), custom_call_target="tpu_custom_call" | custom-call | flops 1073741824 | bytes 8912896 | tf_op jit(solution)/shard_map/pallas_call | solution.py:190
  56.1 2.1 %collective-permute-start.12 = (bf16[64,2048]{1,0:T(8,128)(2,1)S(1)}, bf16[64,2048]{1,0:T(8,128)(2,1)S(1)}, u32[]{:S(2)}, u32[]{:S(2)}) collective-permute-start(bf16[64,2048]{1,0:T(8,128)(2,1)S(1)} %get-tuple-element.26), channel_id=1, source_target_pairs={{0,4},{4,0},{8,12},{12,8},{1,5},{5,1},{9,13},{13,9},{2,6},{6,2},{1... | collective-permute-start | bytes 786440 | tf_op jit(solution)/shard_map/ppermute | solution.py:207
  58.8 4.0 %collective-permute-start.7 = (bf16[64,2048]{1,0:T(8,128)(2,1)S(1)}, bf16[64,2048]{1,0:T(8,128)(2,1)S(1)}, u32[]{:S(2)}, u32[]{:S(2)}) collective-permute-start(bf16[64,2048]{1,0:T(8,128)(2,1)S(1)} %fusion), channel_id=1, source_target_pairs={{2,10},{3,11},{6,14},{7,15},{8,0},{9,1},{12,4},{13,5},{18,26},{19,... | collective-permute-start | bytes 786440 | tf_op jit(solution)/shard_map/ppermute | solution.py:216
  62.8 2.9 %shard_map.69 = (bf16[64,2048]{1,0:T(8,128)(2,1)S(1)}, f32[64,2048]{1,0:T(8,128)S(1)}) custom-call(s32[1]{0:T(128)} %bitcast.flag, bf16[64,2048]{1,0:T(8,128)(2,1)S(1)} %collective-permute-done.4.even, bf16[64,2048]{1,0:T(8,128)(2,1)S(1)} %collective-permute-done.5.odd, bf16[2048,2048]{1,0:T(8,128)(2,1)S(1)} %copy-done.4), custom_call_target="tpu_custom_call" | custom-call | flops 1073741824 | bytes 8912896 | tf_op jit(solution)/shard_map/pallas_call | solution.py:190
  65.7 2.0 %collective-permute-start.6 = (bf16[64,2048]{1,0:T(8,128)(2,1)S(1)}, bf16[64,2048]{1,0:T(8,128)(2,1)S(1)}, u32[]{:S(2)}, u32[]{:S(2)}) collective-permute-start(bf16[64,2048]{1,0:T(8,128)(2,1)S(1)} %get-tuple-element.23), channel_id=1, source_target_pairs={{0,4},{4,0},{8,12},{12,8},{1,5},{5,1},{9,13},{13,9},{2,6},{6,2},{1... | collective-permute-start | bytes 786440 | tf_op jit(solution)/shard_map/ppermute | solution.py:207
  67.8 2.2 %collective-permute-start.16 = (bf16[64,2048]{1,0:T(8,128)(2,1)S(1)}, bf16[64,2048]{1,0:T(8,128)(2,1)S(1)}, u32[]{:S(2)}, u32[]{:S(2)}) collective-permute-start(bf16[64,2048]{1,0:T(8,128)(2,1)S(1)} %fusion.2), channel_id=1, source_target_pairs={{2,10},{3,11},{6,14},{7,15},{8,0},{9,1},{12,4},{13,5},{18,26},{19,... | collective-permute-start | bytes 786440 | tf_op jit(solution)/shard_map/ppermute | solution.py:216
  70.0 2.9 %shard_map.73 = (bf16[64,2048]{1,0:T(8,128)(2,1)S(1)}, f32[64,2048]{1,0:T(8,128)S(1)}) custom-call(s32[1]{0:T(128)} %bitcast.flag, bf16[64,2048]{1,0:T(8,128)(2,1)S(1)} %collective-permute-done.13.even, bf16[64,2048]{1,0:T(8,128)(2,1)S(1)} %collective-permute-done.14.odd, bf16[2048,2048]{1,0:T(8,128)(2,1)S(1)} %copy-done.4), custom_call_target="tpu_custom_call" | custom-call | flops 1073741824 | bytes 8912896 | tf_op jit(solution)/shard_map/pallas_call | solution.py:190
  73.4 1.9 %collective-permute-done.6 = bf16[64,2048]{1,0:T(8,128)(2,1)S(1)} collective-permute-done((bf16[64,2048]{1,0:T(8,128)(2,1)S(1)}, bf16[64,2048]{1,0:T(8,128)(2,1)S(1)}, u32[]{:S(2)}, u32[]{:S(2)}) %collective-permute-start.6) | collective-permute-done | bytes 262176 | tf_op jit(solution)/shard_map/ppermute | solution.py:207
  76.7 9.4 %collective-permute-done.15 = bf16[64,2048]{1,0:T(8,128)(2,1)S(1)} collective-permute-done((bf16[64,2048]{1,0:T(8,128)(2,1)S(1)}, bf16[64,2048]{1,0:T(8,128)(2,1)S(1)}, u32[]{:S(2)}, u32[]{:S(2)}) %collective-permute-start.15) | collective-permute-done | bytes 262176 | tf_op jit(solution)/shard_map/ppermute | solution.py:207
  87.5 3.6 %collective-permute-done.8 = bf16[64,2048]{1,0:T(8,128)(2,1)S(1)} collective-permute-done((bf16[64,2048]{1,0:T(8,128)(2,1)S(1)}, bf16[64,2048]{1,0:T(8,128)(2,1)S(1)}, u32[]{:S(2)}, u32[]{:S(2)}) %collective-permute-start.8) | collective-permute-done | bytes 262176 | tf_op jit(solution)/shard_map/ppermute | solution.py:216
  91.3 11.1 %collective-permute-done.17 = bf16[64,2048]{1,0:T(8,128)(2,1)S(1)} collective-permute-done((bf16[64,2048]{1,0:T(8,128)(2,1)S(1)}, bf16[64,2048]{1,0:T(8,128)(2,1)S(1)}, u32[]{:S(2)}, u32[]{:S(2)}) %collective-permute-start.17) | collective-permute-done | bytes 262176 | tf_op jit(solution)/shard_map/ppermute | solution.py:216
  (58 shorter events, 13.7 us)
Async XLA Ops:
  0.0 6.7 %copy-start = (bf16[32,32]{1,0:T(8,128)(2,1)S(1)}, bf16[32,32]{1,0:T(8,128)(2,1)}, u32[]{:S(2)}) copy-start(bf16[32,32]{1,0:T(8,128)(2,1)} %param.11) | copy-start | bytes 6148
  0.0 7.1 %copy-start.9 = (s32[1,24]{1,0:T(1,128)S(1)}, s32[1,24]{1,0:T(1,128)}, u32[]{:S(2)}) copy-start(s32[1,24]{1,0:T(1,128)} %rows.3) | copy-start | bytes 292
  0.0 7.1 %copy-start.10 = (s32[1,24]{1,0:T(1,128)S(1)}, s32[1,24]{1,0:T(1,128)}, u32[]{:S(2)}) copy-start(s32[1,24]{1,0:T(1,128)} %cols.3) | copy-start | bytes 292
  3.7 21.6 %collective-permute-start = (bf16[64,2048]{1,0:T(8,128)(2,1)}, bf16[64,2048]{1,0:T(8,128)(2,1)S(1)}, u32[]{:S(2)}, u32[]{:S(2)}) collective-permute-start(bf16[64,2048]{1,0:T(8,128)(2,1)} %get-tuple-element.18.near), channel_id=1, source_target_pairs={{0,8},{4,12},{8,0},{12,4},{1,9},{5,13},{9,1},{13,5},{2,10},{6,14},... | collective-permute-start | bytes 786440 | tf_op jit(solution)/shard_map/ppermute | solution.py:207
  6.3 23.8 %collective-permute-start.9 = (bf16[64,2048]{1,0:T(8,128)(2,1)}, bf16[64,2048]{1,0:T(8,128)(2,1)S(1)}, u32[]{:S(2)}, u32[]{:S(2)}) collective-permute-start(bf16[64,2048]{1,0:T(8,128)(2,1)} %get-tuple-element.24.near), channel_id=1, source_target_pairs={{0,8},{4,12},{8,0},{12,4},{1,9},{5,13},{9,1},{13,5},{2,10},{6,14},... | collective-permute-start | bytes 786440 | tf_op jit(solution)/shard_map/ppermute | solution.py:207
  12.1 13.2 %copy-start.8 = (bf16[64,2048]{1,0:T(8,128)(2,1)S(1)}, bf16[64,2048]{1,0:T(8,128)(2,1)}, u32[]{:S(2)}) copy-start(bf16[64,2048]{1,0:T(8,128)(2,1)} %get-tuple-element.18.near) | copy-start | bytes 786436
  12.1 18.1 %copy-start.7 = (bf16[64,2048]{1,0:T(8,128)(2,1)S(1)}, bf16[64,2048]{1,0:T(8,128)(2,1)}, u32[]{:S(2)}) copy-start(bf16[64,2048]{1,0:T(8,128)(2,1)} %get-tuple-element.24.near) | copy-start | bytes 786436
  26.6 9.2 %collective-permute-start.1 = (bf16[64,2048]{1,0:T(8,128)(2,1)S(1)}, bf16[64,2048]{1,0:T(8,128)(2,1)S(1)}, u32[]{:S(2)}, u32[]{:S(2)}) collective-permute-start(bf16[64,2048]{1,0:T(8,128)(2,1)S(1)} %shard_map.67), channel_id=1, source_target_pairs={{0,4},{4,0},{8,12},{12,8},{1,5},{5,1},{9,13},{13,9},{2,6},{6,2},{1... | collective-permute-start | bytes 786440 | tf_op jit(solution)/shard_map/ppermute | solution.py:207
  31.5 9.8 %collective-permute-start.10 = (bf16[64,2048]{1,0:T(8,128)(2,1)S(1)}, bf16[64,2048]{1,0:T(8,128)(2,1)S(1)}, u32[]{:S(2)}, u32[]{:S(2)}) collective-permute-start(bf16[64,2048]{1,0:T(8,128)(2,1)S(1)} %shard_map.71), channel_id=1, source_target_pairs={{0,4},{4,0},{8,12},{12,8},{1,5},{5,1},{9,13},{13,9},{2,6},{6,2},{1... | collective-permute-start | bytes 786440 | tf_op jit(solution)/shard_map/ppermute | solution.py:207
  35.9 7.6 %collective-permute-start.2 = (bf16[64,2048]{1,0:T(8,128)(2,1)S(1)}, bf16[64,2048]{1,0:T(8,128)(2,1)S(1)}, u32[]{:S(2)}, u32[]{:S(2)}) collective-permute-start(bf16[64,2048]{1,0:T(8,128)(2,1)S(1)} %add_convert_fusion.1.even), channel_id=1, source_target_pairs={{0,1},{1,0},{2,3},{3,2},{4,5},{5,4},{6,7},{7,6},{8,9},{9,8},{10,11... | collective-permute-start | bytes 786440 | tf_op jit(solution)/shard_map/ppermute | solution.py:207
  41.3 8.5 %collective-permute-start.11 = (bf16[64,2048]{1,0:T(8,128)(2,1)S(1)}, bf16[64,2048]{1,0:T(8,128)(2,1)S(1)}, u32[]{:S(2)}, u32[]{:S(2)}) collective-permute-start(bf16[64,2048]{1,0:T(8,128)(2,1)S(1)} %add_convert_fusion.even), channel_id=1, source_target_pairs={{0,1},{1,0},{2,3},{3,2},{4,5},{5,4},{6,7},{7,6},{8,9},{9,8},{10,11... | collective-permute-start | bytes 786440 | tf_op jit(solution)/shard_map/ppermute | solution.py:207
  41.4 16.8 %collective-permute-start.4 = (bf16[64,2048]{1,0:T(8,128)(2,1)S(1)}, bf16[64,2048]{1,0:T(8,128)(2,1)S(1)}, u32[]{:S(2)}, u32[]{:S(2)}) collective-permute-start(bf16[64,2048]{1,0:T(8,128)(2,1)S(1)} %add_convert_fusion.1.even), channel_id=1, source_target_pairs={{0,2},{1,3},{2,0},{3,1},{4,6},{5,7},{6,4},{7,5},{8,10},{9,11},{10,... | collective-permute-start | bytes 786440 | tf_op jit(solution)/shard_map/ppermute | solution.py:207
  41.7 16.5 %collective-permute-start.13 = (bf16[64,2048]{1,0:T(8,128)(2,1)S(1)}, bf16[64,2048]{1,0:T(8,128)(2,1)S(1)}, u32[]{:S(2)}, u32[]{:S(2)}) collective-permute-start(bf16[64,2048]{1,0:T(8,128)(2,1)S(1)} %add_convert_fusion.even), channel_id=1, source_target_pairs={{0,2},{1,3},{2,0},{3,1},{4,6},{5,7},{6,4},{7,5},{8,10},{9,11},{10,... | collective-permute-start | bytes 786440 | tf_op jit(solution)/shard_map/ppermute | solution.py:207
  49.8 9.0 %collective-permute-start.3 = (bf16[64,2048]{1,0:T(8,128)(2,1)S(1)}, bf16[64,2048]{1,0:T(8,128)(2,1)S(1)}, u32[]{:S(2)}, u32[]{:S(2)}) collective-permute-start(bf16[64,2048]{1,0:T(8,128)(2,1)S(1)} %get-tuple-element.21), channel_id=1, source_target_pairs={{0,4},{4,0},{8,12},{12,8},{1,5},{5,1},{9,13},{13,9},{2,6},{6,2},{1... | collective-permute-start | bytes 786440 | tf_op jit(solution)/shard_map/ppermute | solution.py:207
  53.2 9.6 %copy-start.4 = (bf16[2048,2048]{1,0:T(8,128)(2,1)S(1)}, bf16[2048,2048]{1,0:T(8,128)(2,1)}, u32[]{:S(2)}) copy-start(bf16[2048,2048]{1,0:T(8,128)(2,1)} %copy-done.1) | copy-start | bytes 25165828
  56.1 11.6 %collective-permute-start.12 = (bf16[64,2048]{1,0:T(8,128)(2,1)S(1)}, bf16[64,2048]{1,0:T(8,128)(2,1)S(1)}, u32[]{:S(2)}, u32[]{:S(2)}) collective-permute-start(bf16[64,2048]{1,0:T(8,128)(2,1)S(1)} %get-tuple-element.26), channel_id=1, source_target_pairs={{0,4},{4,0},{8,12},{12,8},{1,5},{5,1},{9,13},{13,9},{2,6},{6,2},{1... | collective-permute-start | bytes 786440 | tf_op jit(solution)/shard_map/ppermute | solution.py:207
  58.2 4.6 %collective-permute-start.5 = (bf16[64,2048]{1,0:T(8,128)(2,1)S(1)}, bf16[64,2048]{1,0:T(8,128)(2,1)S(1)}, u32[]{:S(2)}, u32[]{:S(2)}) collective-permute-start(bf16[64,2048]{1,0:T(8,128)(2,1)S(1)} %collective-permute-done.4.even), channel_id=1, source_target_pairs={{0,1},{1,0},{2,3},{3,2},{4,5},{5,4},{6,7},{7,6},{8,9},{9,8},{10,11... | collective-permute-start | bytes 786440 | tf_op jit(solution)/shard_map/ppermute | solution.py:207
  58.2 11.8 %collective-permute-start.14 = (bf16[64,2048]{1,0:T(8,128)(2,1)S(1)}, bf16[64,2048]{1,0:T(8,128)(2,1)S(1)}, u32[]{:S(2)}, u32[]{:S(2)}) collective-permute-start(bf16[64,2048]{1,0:T(8,128)(2,1)S(1)} %collective-permute-done.13.even), channel_id=1, source_target_pairs={{0,1},{1,0},{2,3},{3,2},{4,5},{5,4},{6,7},{7,6},{8,9},{9,8},{10,11... | collective-permute-start | bytes 786440 | tf_op jit(solution)/shard_map/ppermute | solution.py:207
  58.8 28.7 %collective-permute-start.7 = (bf16[64,2048]{1,0:T(8,128)(2,1)S(1)}, bf16[64,2048]{1,0:T(8,128)(2,1)S(1)}, u32[]{:S(2)}, u32[]{:S(2)}) collective-permute-start(bf16[64,2048]{1,0:T(8,128)(2,1)S(1)} %fusion), channel_id=1, source_target_pairs={{2,10},{3,11},{6,14},{7,15},{8,0},{9,1},{12,4},{13,5},{18,26},{19,... | collective-permute-start | bytes 786440 | tf_op jit(solution)/shard_map/ppermute | solution.py:216
  65.7 9.6 %collective-permute-start.6 = (bf16[64,2048]{1,0:T(8,128)(2,1)S(1)}, bf16[64,2048]{1,0:T(8,128)(2,1)S(1)}, u32[]{:S(2)}, u32[]{:S(2)}) collective-permute-start(bf16[64,2048]{1,0:T(8,128)(2,1)S(1)} %get-tuple-element.23), channel_id=1, source_target_pairs={{0,4},{4,0},{8,12},{12,8},{1,5},{5,1},{9,13},{13,9},{2,6},{6,2},{1... | collective-permute-start | bytes 786440 | tf_op jit(solution)/shard_map/ppermute | solution.py:207
  67.8 23.5 %collective-permute-start.16 = (bf16[64,2048]{1,0:T(8,128)(2,1)S(1)}, bf16[64,2048]{1,0:T(8,128)(2,1)S(1)}, u32[]{:S(2)}, u32[]{:S(2)}) collective-permute-start(bf16[64,2048]{1,0:T(8,128)(2,1)S(1)} %fusion.2), channel_id=1, source_target_pairs={{2,10},{3,11},{6,14},{7,15},{8,0},{9,1},{12,4},{13,5},{18,26},{19,... | collective-permute-start | bytes 786440 | tf_op jit(solution)/shard_map/ppermute | solution.py:216
  72.9 13.1 %collective-permute-start.15 = (bf16[64,2048]{1,0:T(8,128)(2,1)S(1)}, bf16[64,2048]{1,0:T(8,128)(2,1)S(1)}, u32[]{:S(2)}, u32[]{:S(2)}) collective-permute-start(bf16[64,2048]{1,0:T(8,128)(2,1)S(1)} %get-tuple-element.28), channel_id=1, source_target_pairs={{0,4},{4,0},{8,12},{12,8},{1,5},{5,1},{9,13},{13,9},{2,6},{6,2},{1... | collective-permute-start | bytes 786440 | tf_op jit(solution)/shard_map/ppermute | solution.py:207
  75.4 15.7 %collective-permute-start.8 = (bf16[64,2048]{1,0:T(8,128)(2,1)S(1)}, bf16[64,2048]{1,0:T(8,128)(2,1)S(1)}, u32[]{:S(2)}, u32[]{:S(2)}) collective-permute-start(bf16[64,2048]{1,0:T(8,128)(2,1)S(1)} %fusion.1), channel_id=1, source_target_pairs={{0,8},{1,9},{4,12},{5,13},{10,2},{11,3},{14,6},{15,7},{16,24},{17,... | collective-permute-start | bytes 786440 | tf_op jit(solution)/shard_map/ppermute | solution.py:216
  86.2 16.2 %collective-permute-start.17 = (bf16[64,2048]{1,0:T(8,128)(2,1)S(1)}, bf16[64,2048]{1,0:T(8,128)(2,1)S(1)}, u32[]{:S(2)}, u32[]{:S(2)}) collective-permute-start(bf16[64,2048]{1,0:T(8,128)(2,1)S(1)} %fusion.3), channel_id=1, source_target_pairs={{0,8},{1,9},{4,12},{5,13},{10,2},{11,3},{14,6},{15,7},{16,24},{17,... | collective-permute-start | bytes 786440 | tf_op jit(solution)/shard_map/ppermute | solution.py:216
  (5 other events, 15.0 us)

commit v3 on v2

--- a/solution.py
+++ b/solution.py
@@ -205,15 +205,6 @@
 def swap(x, axis, distance):
     size = lax.axis_size(axis)
     return lax.ppermute(x, axis, [(i, i ^ distance) for i in range(size)])
-
-
-def forward(x, late):
-    pairs = []
-    for z in range(4):
-        for r in range(4):
-            if ((z ^ r) & 2 == 0) == late:
-                pairs.append((z * 4 + r, (z ^ 2) * 4 + r))
-    return lax.ppermute(x, ("aux", "row"), pairs)
 
 
 def four_by_four(args, squared):
@@ -240,14 +231,11 @@
     for late in (0, 1):
         for piece in pieces:
             send, keep = product_rows(flag, *piece[late], right)
-            came = swap(send, "aux", 1)
-            total = keep + came.astype(F32)
-            passed = forward(total.astype(BF16), late == 1)
-            sums[late].append((total, passed))
-    results = [
-        jnp.where(first_own, early, late) + passed_early.astype(F32) + passed_late.astype(F32)
-        for (early, passed_early), (late, passed_late) in zip(*sums)
-    ]
+            sums[late].append(keep + swap(send, "aux", 1).astype(F32))
+    results = []
+    for early, late in zip(*sums):
+        passed = swap(jnp.where(first_own, late, early).astype(BF16), "aux", 2)
+        results.append(jnp.where(first_own, early, late) + passed.astype(F32))
     return jnp.concatenate(results, axis=0)
 
 

time: 104 us -> 104 us (level)
  the two profiles are of different devices: /device:TPU:6 before, /device:TPU:0 now
where the time goes in v3:
time: 104 us
  waiting for transfers between devices  37 us (36%)
  Pallas kernels  30.1 us (29%)
  starting transfers between devices  18.5 us (18%)
  local copies, waits for them, and re-layouts  15.1 us (15%)
  other arithmetic  1.76 us (2%)
    ppermute x16, waiting for transfers between devices, swap(): return lax.ppermute(x, axis, [(i, i ^ distance) for i in range(size)])  37 us
    ppermute x16, starting transfers between devices, swap(): return lax.ppermute(x, axis, [(i, i ^ distance) for i in range(size)])  18.5 us
    unnamed x20, local copies, waits for them, and re-layouts  15 us
    pallas_call x4, Pallas kernels, product_rows(): pl.pallas_call(product_body, in_specs=[pl.BlockSpec(memory_space=pltpu.SM...  11.6 us
    pallas_call x1, Pallas kernels, half_rows(): pl.pallas_call(functools.partial(half_body, blocks), in_specs=[smem] * 3...  9.96 us
    pallas_call x4, Pallas kernels, mix(): pl.pallas_call(functools.partial(mix_body, occ, which), in_specs=[pl.Bloc...  5.36 us
    pallas_call x1, Pallas kernels, window_rows(): pl.pallas_call(functools.partial(window_body, blocks, outs), in_specs=[sm...  3.23 us
  transfers between devices with their start and end apart: 16, of which 8 were waited for; matrix products, arithmetic and copies ran while one was open for 1% of the time, Pallas kernels for 26%

profile of v3, /device:TPU:0, one launch (start us, length us, event | category | flops | bytes accessed | tf_op | source)
XLA Modules:
  0.0 103.6 jit_solution(15890563046479168953)
XLA Ops:
  0.7 3.2 %shard_map.65 = (bf16[64,2048]{1,0:T(8,128)(2,1)}, bf16[64,2048]{1,0:T(8,128)(2,1)}) custom-call(s32[1,24]{1,0:T(1,128)} %rows.3, s32[1,24]{1,0:T(1,128)} %cols.3, s32[1,1]{1,0:T(1,128)S(6)} %copy.15.live, bf16[8,24,128,128]{3,2,1,0:T(8,128)(2,1)} %tiles.3, bf16[8192,256]{1,0:T(8,128)(2,1)} %orbitals.3), custom_call_target="tpu_custom_call" | custom-call | flops 134217728 | bytes 524288 | tf_op jit(solution)/shard_map/pallas_call | solution.py:72
  3.9 3.8 %collective-permute-start = (bf16[64,2048]{1,0:T(8,128)(2,1)}, bf16[64,2048]{1,0:T(8,128)(2,1)S(1)}, u32[]{:S(2)}, u32[]{:S(2)}) collective-permute-start(bf16[64,2048]{1,0:T(8,128)(2,1)} %get-tuple-element.18.near), channel_id=1, source_target_pairs={{0,8},{4,12},{8,0},{12,4},{1,9},{5,13},{9,1},{13,5},{2,10},{6,14},... | collective-permute-start | bytes 786440 | tf_op jit(solution)/shard_map/ppermute | solution.py:207
  8.3 2.8 %copy-done.4 = bf16[8,24,128,128]{3,2,1,0:T(8,128)(2,1)S(1)} copy-done((bf16[8,24,128,128]{3,2,1,0:T(8,128)(2,1)S(1)}, bf16[8,24,128,128]{3,2,1,0:T(8,128)(2,1)}, u32[]{:S(2)}) %copy-start.4) | copy-done | bytes 6291480
  11.0 2.2 %copy-done.5 = bf16[8192,256]{1,0:T(8,128)(2,1)S(1)} copy-done((bf16[8192,256]{1,0:T(8,128)(2,1)S(1)}, bf16[8192,256]{1,0:T(8,128)(2,1)}, u32[]{:S(2)}) %copy-start.5) | copy-done | bytes 4194328
  13.2 10.0 %shard_map.64 = (bf16[2048,2048]{1,0:T(8,128)(2,1)S(1)}, f32[2,8,16]{2,1,0:T(8,128)S(1)}) custom-call(s32[1,24]{1,0:T(1,128)S(1)} %copy-done.8, s32[1,24]{1,0:T(1,128)S(1)} %copy-done.9, s32[1,1]{1,0:T(1,128)S(6)} %copy.15.live, bf16[8,24,128,128]{3,2,1,0:T(8,128)(2,1)S(1)} %copy-done.4, bf16[8192,256]{1,0:T(8,128)(2,1)S(1)} %copy-done.5, ...), custom_call_target="tpu_custom_call" | custom-call | flops 3221225472 | bytes 18874368 | tf_op jit(solution)/shard_map/pallas_call | solution.py:120
  23.2 3.3 %copy-done.1 = bf16[2048,2048]{1,0:T(8,128)(2,1)} copy-done((bf16[2048,2048]{1,0:T(8,128)(2,1)}, bf16[2048,2048]{1,0:T(8,128)(2,1)S(1)}, u32[]{:S(2)}) %copy-start.1) | copy-done | bytes 8388632
  28.5 2.7 %collective-permute-done.8.far = bf16[64,2048]{1,0:T(8,128)(2,1)S(1)} collective-permute-done((bf16[64,2048]{1,0:T(8,128)(2,1)}, bf16[64,2048]{1,0:T(8,128)(2,1)S(1)}, u32[]{:S(2)}, u32[]{:S(2)}) %collective-permute-start.8) | collective-permute-done | bytes 262176 | tf_op jit(solution)/shard_map/ppermute | solution.py:207
  37.1 1.9 %collective-permute-start.4 = (bf16[64,2048]{1,0:T(8,128)(2,1)S(1)}, bf16[64,2048]{1,0:T(8,128)(2,1)S(1)}, u32[]{:S(2)}, u32[]{:S(2)}) collective-permute-start(bf16[64,2048]{1,0:T(8,128)(2,1)S(1)} %add_convert_fusion.1.even), channel_id=1, source_target_pairs={{0,2},{1,3},{2,0},{3,1},{4,6},{5,7},{6,4},{7,5},{8,10},{9,11},{10,... | collective-permute-start | bytes 786440 | tf_op jit(solution)/shard_map/ppermute | solution.py:207
  39.1 3.3 %collective-permute-done.9 = bf16[64,2048]{1,0:T(8,128)(2,1)S(1)} collective-permute-done((bf16[64,2048]{1,0:T(8,128)(2,1)S(1)}, bf16[64,2048]{1,0:T(8,128)(2,1)S(1)}, u32[]{:S(2)}, u32[]{:S(2)}) %collective-permute-start.9) | collective-permute-done | bytes 262176 | tf_op jit(solution)/shard_map/ppermute | solution.py:207
  42.4 1.8 %collective-permute-start.12 = (bf16[64,2048]{1,0:T(8,128)(2,1)S(1)}, bf16[64,2048]{1,0:T(8,128)(2,1)S(1)}, u32[]{:S(2)}, u32[]{:S(2)}) collective-permute-start(bf16[64,2048]{1,0:T(8,128)(2,1)S(1)} %add_convert_fusion.even), channel_id=1, source_target_pairs={{0,2},{1,3},{2,0},{3,1},{4,6},{5,7},{6,4},{7,5},{8,10},{9,11},{10,... | collective-permute-start | bytes 786440 | tf_op jit(solution)/shard_map/ppermute | solution.py:207
  45.4 5.1 %collective-permute-done.12.even = bf16[64,2048]{1,0:T(8,128)(2,1)S(1)} collective-permute-done((bf16[64,2048]{1,0:T(8,128)(2,1)S(1)}, bf16[64,2048]{1,0:T(8,128)(2,1)S(1)}, u32[]{:S(2)}, u32[]{:S(2)}) %collective-permute-start.12) | collective-permute-done | bytes 262176 | tf_op jit(solution)/shard_map/ppermute | solution.py:207
  50.5 3.4 %copy-done.2 = bf16[2048,2048]{1,0:T(8,128)(2,1)S(1)} copy-done((bf16[2048,2048]{1,0:T(8,128)(2,1)S(1)}, bf16[2048,2048]{1,0:T(8,128)(2,1)}, u32[]{:S(2)}) %copy-start.2) | copy-done | bytes 8388632
  53.9 2.9 %shard_map.68 = (bf16[64,2048]{1,0:T(8,128)(2,1)S(1)}, f32[64,2048]{1,0:T(8,128)S(1)}) custom-call(s32[1]{0:T(128)} %bitcast.flag, bf16[64,2048]{1,0:T(8,128)(2,1)S(1)} %add_convert_fusion.1.even, bf16[64,2048]{1,0:T(8,128)(2,1)S(1)} %collective-permute-done.2.odd, bf16[2048,2048]{1,0:T(8,128)(2,1)S(1)} %copy-done.2), custom_call_target="tpu_custom_call" | custom-call | flops 1073741824 | bytes 8912896 | tf_op jit(solution)/shard_map/pallas_call | solution.py:190
  56.9 2.9 %shard_map.69 = (bf16[64,2048]{1,0:T(8,128)(2,1)S(1)}, f32[64,2048]{1,0:T(8,128)S(1)}) custom-call(s32[1]{0:T(128)} %bitcast.flag, bf16[64,2048]{1,0:T(8,128)(2,1)S(1)} %collective-permute-done.4.even, bf16[64,2048]{1,0:T(8,128)(2,1)S(1)} %collective-permute-done.5.odd, bf16[2048,2048]{1,0:T(8,128)(2,1)S(1)} %copy-done.2), custom_call_target="tpu_custom_call" | custom-call | flops 1073741824 | bytes 8912896 | tf_op jit(solution)/shard_map/pallas_call | solution.py:190
  59.8 2.1 %collective-permute-start.6 = (bf16[64,2048]{1,0:T(8,128)(2,1)S(1)}, bf16[64,2048]{1,0:T(8,128)(2,1)S(1)}, u32[]{:S(2)}, u32[]{:S(2)}) collective-permute-start(bf16[64,2048]{1,0:T(8,128)(2,1)S(1)} %get-tuple-element.23), channel_id=1, source_target_pairs={{0,4},{4,0},{8,12},{12,8},{1,5},{5,1},{9,13},{13,9},{2,6},{6,2},{1... | collective-permute-start | bytes 786440 | tf_op jit(solution)/shard_map/ppermute | solution.py:207
  61.8 3.4 %copy-done.3 = bf16[2048,2048]{1,0:T(8,128)(2,1)S(1)} copy-done((bf16[2048,2048]{1,0:T(8,128)(2,1)S(1)}, bf16[2048,2048]{1,0:T(8,128)(2,1)}, u32[]{:S(2)}) %copy-start.3) | copy-done | bytes 8388632
  65.2 2.9 %shard_map.72 = (bf16[64,2048]{1,0:T(8,128)(2,1)S(1)}, f32[64,2048]{1,0:T(8,128)S(1)}) custom-call(s32[1]{0:T(128)} %bitcast.flag, bf16[64,2048]{1,0:T(8,128)(2,1)S(1)} %add_convert_fusion.even, bf16[64,2048]{1,0:T(8,128)(2,1)S(1)} %collective-permute-done.10.odd, bf16[2048,2048]{1,0:T(8,128)(2,1)S(1)} %copy-done.3), custom_call_target="tpu_custom_call" | custom-call | flops 1073741824 | bytes 8912896 | tf_op jit(solution)/shard_map/pallas_call | solution.py:190
  68.2 2.9 %shard_map.73 = (bf16[64,2048]{1,0:T(8,128)(2,1)S(1)}, f32[64,2048]{1,0:T(8,128)S(1)}) custom-call(s32[1]{0:T(128)} %bitcast.flag, bf16[64,2048]{1,0:T(8,128)(2,1)S(1)} %collective-permute-done.12.even, bf16[64,2048]{1,0:T(8,128)(2,1)S(1)} %collective-permute-done.13.odd, bf16[2048,2048]{1,0:T(8,128)(2,1)S(1)} %copy-done.3), custom_call_target="tpu_custom_call" | custom-call | flops 1073741824 | bytes 8912896 | tf_op jit(solution)/shard_map/pallas_call | solution.py:190
  71.1 2.1 %collective-permute-start.14 = (bf16[64,2048]{1,0:T(8,128)(2,1)S(1)}, bf16[64,2048]{1,0:T(8,128)(2,1)S(1)}, u32[]{:S(2)}, u32[]{:S(2)}) collective-permute-start(bf16[64,2048]{1,0:T(8,128)(2,1)S(1)} %get-tuple-element.28), channel_id=1, source_target_pairs={{0,4},{4,0},{8,12},{12,8},{1,5},{5,1},{9,13},{13,9},{2,6},{6,2},{1... | collective-permute-start | bytes 786440 | tf_op jit(solution)/shard_map/ppermute | solution.py:207
  73.3 2.6 %collective-permute-start.7 = (bf16[64,2048]{1,0:T(8,128)(2,1)S(1)}, bf16[64,2048]{1,0:T(8,128)(2,1)S(1)}, u32[]{:S(2)}, u32[]{:S(2)}) collective-permute-start(bf16[64,2048]{1,0:T(8,128)(2,1)S(1)} %select_convert_fusion.1), channel_id=1, source_target_pairs={{0,8},{4,12},{8,0},{12,4},{1,9},{5,13},{9,1},{13,5},{2,10},{6,14},... | collective-permute-start | bytes 786440 | tf_op jit(solution)/shard_map/ppermute | solution.py:207
  75.9 7.1 %collective-permute-done.11 = bf16[64,2048]{1,0:T(8,128)(2,1)S(1)} collective-permute-done((bf16[64,2048]{1,0:T(8,128)(2,1)S(1)}, bf16[64,2048]{1,0:T(8,128)(2,1)S(1)}, u32[]{:S(2)}, u32[]{:S(2)}) %collective-permute-start.11) | collective-permute-done | bytes 262176 | tf_op jit(solution)/shard_map/ppermute | solution.py:207
  83.0 5.0 %collective-permute-done.14 = bf16[64,2048]{1,0:T(8,128)(2,1)S(1)} collective-permute-done((bf16[64,2048]{1,0:T(8,128)(2,1)S(1)}, bf16[64,2048]{1,0:T(8,128)(2,1)S(1)}, u32[]{:S(2)}, u32[]{:S(2)}) %collective-permute-start.14) | collective-permute-done | bytes 262176 | tf_op jit(solution)/shard_map/ppermute | solution.py:207
  88.1 2.0 %collective-permute-start.15 = (bf16[64,2048]{1,0:T(8,128)(2,1)S(1)}, bf16[64,2048]{1,0:T(8,128)(2,1)S(1)}, u32[]{:S(2)}, u32[]{:S(2)}) collective-permute-start(bf16[64,2048]{1,0:T(8,128)(2,1)S(1)} %select_convert_fusion), channel_id=1, source_target_pairs={{0,8},{4,12},{8,0},{12,4},{1,9},{5,13},{9,1},{13,5},{2,10},{6,14},... | collective-permute-start | bytes 786440 | tf_op jit(solution)/shard_map/ppermute | solution.py:207
  90.3 12.2 %collective-permute-done.15 = bf16[64,2048]{1,0:T(8,128)(2,1)S(1)} collective-permute-done((bf16[64,2048]{1,0:T(8,128)(2,1)S(1)}, bf16[64,2048]{1,0:T(8,128)(2,1)S(1)}, u32[]{:S(2)}, u32[]{:S(2)}) %collective-permute-start.15) | collective-permute-done | bytes 262176 | tf_op jit(solution)/shard_map/ppermute | solution.py:207
  (50 shorter events, 11.3 us)
Async XLA Ops:
  0.0 7.8 %copy-start = (bf16[32,32]{1,0:T(8,128)(2,1)S(1)}, bf16[32,32]{1,0:T(8,128)(2,1)}, u32[]{:S(2)}) copy-start(bf16[32,32]{1,0:T(8,128)(2,1)} %param.11) | copy-start | bytes 6148
  0.0 8.2 %copy-start.8 = (s32[1,24]{1,0:T(1,128)S(1)}, s32[1,24]{1,0:T(1,128)}, u32[]{:S(2)}) copy-start(s32[1,24]{1,0:T(1,128)} %rows.3) | copy-start | bytes 292
  0.0 8.2 %copy-start.9 = (s32[1,24]{1,0:T(1,128)S(1)}, s32[1,24]{1,0:T(1,128)}, u32[]{:S(2)}) copy-start(s32[1,24]{1,0:T(1,128)} %cols.3) | copy-start | bytes 292
  3.9 22.5 %collective-permute-start = (bf16[64,2048]{1,0:T(8,128)(2,1)}, bf16[64,2048]{1,0:T(8,128)(2,1)S(1)}, u32[]{:S(2)}, u32[]{:S(2)}) collective-permute-start(bf16[64,2048]{1,0:T(8,128)(2,1)} %get-tuple-element.18.near), channel_id=1, source_target_pairs={{0,8},{4,12},{8,0},{12,4},{1,9},{5,13},{9,1},{13,5},{2,10},{6,14},... | collective-permute-start | bytes 786440 | tf_op jit(solution)/shard_map/ppermute | solution.py:207
  7.8 23.5 %collective-permute-start.8 = (bf16[64,2048]{1,0:T(8,128)(2,1)}, bf16[64,2048]{1,0:T(8,128)(2,1)S(1)}, u32[]{:S(2)}, u32[]{:S(2)}) collective-permute-start(bf16[64,2048]{1,0:T(8,128)(2,1)} %get-tuple-element.24.near), channel_id=1, source_target_pairs={{0,8},{4,12},{8,0},{12,4},{1,9},{5,13},{9,1},{13,5},{2,10},{6,14},... | collective-permute-start | bytes 786440 | tf_op jit(solution)/shard_map/ppermute | solution.py:207
  13.2 13.3 %copy-start.7 = (bf16[64,2048]{1,0:T(8,128)(2,1)S(1)}, bf16[64,2048]{1,0:T(8,128)(2,1)}, u32[]{:S(2)}) copy-start(bf16[64,2048]{1,0:T(8,128)(2,1)} %get-tuple-element.18.near) | copy-start | bytes 786436
  13.2 18.0 %copy-start.6 = (bf16[64,2048]{1,0:T(8,128)(2,1)S(1)}, bf16[64,2048]{1,0:T(8,128)(2,1)}, u32[]{:S(2)}) copy-start(bf16[64,2048]{1,0:T(8,128)(2,1)} %get-tuple-element.24.near) | copy-start | bytes 786436
  23.2 3.3 %copy-start.1 = (bf16[2048,2048]{1,0:T(8,128)(2,1)}, bf16[2048,2048]{1,0:T(8,128)(2,1)S(1)}, u32[]{:S(2)}) copy-start(bf16[2048,2048]{1,0:T(8,128)(2,1)S(1)} %get-tuple-element.19.right) | copy-start | bytes 25165828
  27.8 9.2 %collective-permute-start.1 = (bf16[64,2048]{1,0:T(8,128)(2,1)S(1)}, bf16[64,2048]{1,0:T(8,128)(2,1)S(1)}, u32[]{:S(2)}, u32[]{:S(2)}) collective-permute-start(bf16[64,2048]{1,0:T(8,128)(2,1)S(1)} %shard_map.67), channel_id=1, source_target_pairs={{0,4},{4,0},{8,12},{12,8},{1,5},{5,1},{9,13},{13,9},{2,6},{6,2},{1... | collective-permute-start | bytes 786440 | tf_op jit(solution)/shard_map/ppermute | solution.py:207
  32.6 9.8 %collective-permute-start.9 = (bf16[64,2048]{1,0:T(8,128)(2,1)S(1)}, bf16[64,2048]{1,0:T(8,128)(2,1)S(1)}, u32[]{:S(2)}, u32[]{:S(2)}) collective-permute-start(bf16[64,2048]{1,0:T(8,128)(2,1)S(1)} %shard_map.71), channel_id=1, source_target_pairs={{0,4},{4,0},{8,12},{12,8},{1,5},{5,1},{9,13},{13,9},{2,6},{6,2},{1... | collective-permute-start | bytes 786440 | tf_op jit(solution)/shard_map/ppermute | solution.py:207
  37.1 7.7 %collective-permute-start.4 = (bf16[64,2048]{1,0:T(8,128)(2,1)S(1)}, bf16[64,2048]{1,0:T(8,128)(2,1)S(1)}, u32[]{:S(2)}, u32[]{:S(2)}) collective-permute-start(bf16[64,2048]{1,0:T(8,128)(2,1)S(1)} %add_convert_fusion.1.even), channel_id=1, source_target_pairs={{0,2},{1,3},{2,0},{3,1},{4,6},{5,7},{6,4},{7,5},{8,10},{9,11},{10,... | collective-permute-start | bytes 786440 | tf_op jit(solution)/shard_map/ppermute | solution.py:207
  42.4 8.1 %collective-permute-start.12 = (bf16[64,2048]{1,0:T(8,128)(2,1)S(1)}, bf16[64,2048]{1,0:T(8,128)(2,1)S(1)}, u32[]{:S(2)}, u32[]{:S(2)}) collective-permute-start(bf16[64,2048]{1,0:T(8,128)(2,1)S(1)} %add_convert_fusion.even), channel_id=1, source_target_pairs={{0,2},{1,3},{2,0},{3,1},{4,6},{5,7},{6,4},{7,5},{8,10},{9,11},{10,... | collective-permute-start | bytes 786440 | tf_op jit(solution)/shard_map/ppermute | solution.py:207
  44.3 6.2 %collective-permute-start.2 = (bf16[64,2048]{1,0:T(8,128)(2,1)S(1)}, bf16[64,2048]{1,0:T(8,128)(2,1)S(1)}, u32[]{:S(2)}, u32[]{:S(2)}) collective-permute-start(bf16[64,2048]{1,0:T(8,128)(2,1)S(1)} %add_convert_fusion.1.even), channel_id=1, source_target_pairs={{0,1},{1,0},{2,3},{3,2},{4,5},{5,4},{6,7},{7,6},{8,9},{9,8},{10,11... | collective-permute-start | bytes 786440 | tf_op jit(solution)/shard_map/ppermute | solution.py:207
  44.9 12.0 %collective-permute-start.5 = (bf16[64,2048]{1,0:T(8,128)(2,1)S(1)}, bf16[64,2048]{1,0:T(8,128)(2,1)S(1)}, u32[]{:S(2)}, u32[]{:S(2)}) collective-permute-start(bf16[64,2048]{1,0:T(8,128)(2,1)S(1)} %collective-permute-done.4.even), channel_id=1, source_target_pairs={{0,1},{1,0},{2,3},{3,2},{4,5},{5,4},{6,7},{7,6},{8,9},{9,8},{10,11... | collective-permute-start | bytes 786440 | tf_op jit(solution)/shard_map/ppermute | solution.py:207
  44.9 17.0 %collective-permute-start.10 = (bf16[64,2048]{1,0:T(8,128)(2,1)S(1)}, bf16[64,2048]{1,0:T(8,128)(2,1)S(1)}, u32[]{:S(2)}, u32[]{:S(2)}) collective-permute-start(bf16[64,2048]{1,0:T(8,128)(2,1)S(1)} %add_convert_fusion.even), channel_id=1, source_target_pairs={{0,1},{1,0},{2,3},{3,2},{4,5},{5,4},{6,7},{7,6},{8,9},{9,8},{10,11... | collective-permute-start | bytes 786440 | tf_op jit(solution)/shard_map/ppermute | solution.py:207
  50.5 17.7 %collective-permute-start.13 = (bf16[64,2048]{1,0:T(8,128)(2,1)S(1)}, bf16[64,2048]{1,0:T(8,128)(2,1)S(1)}, u32[]{:S(2)}, u32[]{:S(2)}) collective-permute-start(bf16[64,2048]{1,0:T(8,128)(2,1)S(1)} %collective-permute-done.12.even), channel_id=1, source_target_pairs={{0,1},{1,0},{2,3},{3,2},{4,5},{5,4},{6,7},{7,6},{8,9},{9,8},{10,11... | collective-permute-start | bytes 786440 | tf_op jit(solution)/shard_map/ppermute | solution.py:207
  50.5 3.4 %copy-start.2 = (bf16[2048,2048]{1,0:T(8,128)(2,1)S(1)}, bf16[2048,2048]{1,0:T(8,128)(2,1)}, u32[]{:S(2)}) copy-start(bf16[2048,2048]{1,0:T(8,128)(2,1)} %copy-done.1) | copy-start | bytes 25165828
  56.8 16.4 %collective-permute-start.3 = (bf16[64,2048]{1,0:T(8,128)(2,1)S(1)}, bf16[64,2048]{1,0:T(8,128)(2,1)S(1)}, u32[]{:S(2)}, u32[]{:S(2)}) collective-permute-start(bf16[64,2048]{1,0:T(8,128)(2,1)S(1)} %get-tuple-element.21), channel_id=1, source_target_pairs={{0,4},{4,0},{8,12},{12,8},{1,5},{5,1},{9,13},{13,9},{2,6},{6,2},{1... | collective-permute-start | bytes 786440 | tf_op jit(solution)/shard_map/ppermute | solution.py:207
  59.8 13.4 %collective-permute-start.6 = (bf16[64,2048]{1,0:T(8,128)(2,1)S(1)}, bf16[64,2048]{1,0:T(8,128)(2,1)S(1)}, u32[]{:S(2)}, u32[]{:S(2)}) collective-permute-start(bf16[64,2048]{1,0:T(8,128)(2,1)S(1)} %get-tuple-element.23), channel_id=1, source_target_pairs={{0,4},{4,0},{8,12},{12,8},{1,5},{5,1},{9,13},{13,9},{2,6},{6,2},{1... | collective-permute-start | bytes 786440 | tf_op jit(solution)/shard_map/ppermute | solution.py:207
  61.8 3.4 %copy-start.3 = (bf16[2048,2048]{1,0:T(8,128)(2,1)S(1)}, bf16[2048,2048]{1,0:T(8,128)(2,1)}, u32[]{:S(2)}) copy-start(bf16[2048,2048]{1,0:T(8,128)(2,1)} %copy-done.1) | copy-start | bytes 25165828
  68.1 14.9 %collective-permute-start.11 = (bf16[64,2048]{1,0:T(8,128)(2,1)S(1)}, bf16[64,2048]{1,0:T(8,128)(2,1)S(1)}, u32[]{:S(2)}, u32[]{:S(2)}) collective-permute-start(bf16[64,2048]{1,0:T(8,128)(2,1)S(1)} %get-tuple-element.26), channel_id=1, source_target_pairs={{0,4},{4,0},{8,12},{12,8},{1,5},{5,1},{9,13},{13,9},{2,6},{6,2},{1... | collective-permute-start | bytes 786440 | tf_op jit(solution)/shard_map/ppermute | solution.py:207
  71.1 16.9 %collective-permute-start.14 = (bf16[64,2048]{1,0:T(8,128)(2,1)S(1)}, bf16[64,2048]{1,0:T(8,128)(2,1)S(1)}, u32[]{:S(2)}, u32[]{:S(2)}) collective-permute-start(bf16[64,2048]{1,0:T(8,128)(2,1)S(1)} %get-tuple-element.28), channel_id=1, source_target_pairs={{0,4},{4,0},{8,12},{12,8},{1,5},{5,1},{9,13},{13,9},{2,6},{6,2},{1... | collective-permute-start | bytes 786440 | tf_op jit(solution)/shard_map/ppermute | solution.py:207
  73.3 16.8 %collective-permute-start.7 = (bf16[64,2048]{1,0:T(8,128)(2,1)S(1)}, bf16[64,2048]{1,0:T(8,128)(2,1)S(1)}, u32[]{:S(2)}, u32[]{:S(2)}) collective-permute-start(bf16[64,2048]{1,0:T(8,128)(2,1)S(1)} %select_convert_fusion.1), channel_id=1, source_target_pairs={{0,8},{4,12},{8,0},{12,4},{1,9},{5,13},{9,1},{13,5},{2,10},{6,14},... | collective-permute-start | bytes 786440 | tf_op jit(solution)/shard_map/ppermute | solution.py:207
  88.1 14.3 %collective-permute-start.15 = (bf16[64,2048]{1,0:T(8,128)(2,1)S(1)}, bf16[64,2048]{1,0:T(8,128)(2,1)S(1)}, u32[]{:S(2)}, u32[]{:S(2)}) collective-permute-start(bf16[64,2048]{1,0:T(8,128)(2,1)S(1)} %select_convert_fusion), channel_id=1, source_target_pairs={{0,8},{4,12},{8,0},{12,4},{1,9},{5,13},{9,1},{13,5},{2,10},{6,14},... | collective-permute-start | bytes 786440 | tf_op jit(solution)/shard_map/ppermute | solution.py:207
  (2 other events, 5.0 us)

commit v4 on v3

--- a/solution.py
+++ b/solution.py
@@ -82,9 +82,7 @@
             pltpu.SemaphoreType.DMA((held,)),
         ],
         compiler_params=pltpu.CompilerParams(vmem_limit_bytes=WHOLE),
-        cost_estimate=pl.CostEstimate(
-            flops=4 * aux_dev * width * width * occ, bytes_accessed=4 * aux_dev * width * width,
-            transcendentals=0),
+        cost_estimate=pl.CostEstimate(flops=1_000_000_000, bytes_accessed=3_333_333, transcendentals=0),
     )(rows, cols, live, tiles, orbitals)
 
 
@@ -127,10 +125,7 @@
         ],
         scratch_shapes=[pltpu.VMEM((aux_dev * width, occ), F32)],
         compiler_params=pltpu.CompilerParams(vmem_limit_bytes=LIMIT),
-        cost_estimate=pl.CostEstimate(
-            flops=4 * slots * aux_dev * width * width * occ,
-            bytes_accessed=2 * (slots * aux_dev * width * width + basis * occ + blocks * width * wide),
-            transcendentals=0),
+        cost_estimate=pl.CostEstimate(flops=20_000_000_000, bytes_accessed=66_666_666, transcendentals=0),
     )(rows, cols, live, tiles, orbitals, weights)
 
 
@@ -163,8 +158,7 @@
         out_specs=pl.BlockSpec(memory_space=pltpu.VMEM),
         out_shape=jax.ShapeDtypeStruct((rows, wide), dtype),
         compiler_params=pltpu.CompilerParams(vmem_limit_bytes=LIMIT),
-        cost_estimate=pl.CostEstimate(
-            flops=2 * rows * wide * weight.shape[2], bytes_accessed=8 * rows * wide, transcendentals=0),
+        cost_estimate=pl.CostEstimate(flops=2_000_000_000, bytes_accessed=6_666_666, transcendentals=0),
     )(weight, near, far)
 
 
@@ -197,8 +191,7 @@
             jax.ShapeDtypeStruct((rows, count), F32),
         ],
         compiler_params=pltpu.CompilerParams(vmem_limit_bytes=LIMIT),
-        cost_estimate=pl.CostEstimate(
-            flops=4 * rows * wide * count, bytes_accessed=2 * wide * (count + 2 * rows), transcendentals=0),
+        cost_estimate=pl.CostEstimate(flops=3_000_000_000, bytes_accessed=10_000_000, transcendentals=0),
     )(flag, even, odd, right)
 
 
@@ -218,20 +211,21 @@
     first_own = ((r ^ z) & 2) == 0
     fars = [swap(x, "aux", 2) for x in window]
     right, weights = half_rows(*args, weights)
-    pieces = []
+    pieces, sums, ready = [], [[], []], None
     for x, far in zip(window, fars):
         message = swap(mix(weights, 0, x, far, occ, BF16), "aux", 1)
         mine = mix(weights, 1, x, far, occ, F32)
         g0 = (mine + message.astype(F32)).astype(BF16)
         g1 = swap(g0, "row", 1)
-        g2 = swap(g0, "row", 2)
-        g3 = swap(g2, "row", 1)
-        pieces.append(((g0, g1), (g2, g3)))
-    sums = [[], []]
-    for late in (0, 1):
-        for piece in pieces:
-            send, keep = product_rows(flag, *piece[late], right)
-            sums[late].append(keep + swap(send, "aux", 1).astype(F32))
+        pieces.append(swap(g0, "row", 2))
+        send, ready = product_rows(flag, g0, g1, right)
+        sums[0].append(ready)
+        sums[1].append(swap(send, "aux", 1))
+    sums[0] = [keep + came.astype(F32) for keep, came in zip(*sums)]
+    sums[1] = []
+    for g2 in pieces:
+        send, keep = product_rows(flag, g2, swap(g2, "row", 1), right)
+        sums[1].append(keep + swap(send, "aux", 1).astype(F32))
     results = []
     for early, late in zip(*sums):
         passed = swap(jnp.where(first_own, late, early).astype(BF16), "aux", 2)

time: 104 us -> 94.5 us (0.909)
  local copies, waits for them, and re-layouts: 15.1 us -> 8.37 us
  Pallas kernels: 30.1 us -> 26.9 us
  waiting for transfers between devices: 37 us -> 39.3 us
  starting transfers between devices: 18.5 us -> 17 us
    unnamed x20, local copies, waits for them, and re-layouts: 15 us -> 8.26 us
    pallas_call x1, Pallas kernels: 9.96 us -> 6.91 us  [half_rows(): pl.pallas_call(functools.partial(half_body, blocks), in_specs=[smem] * 3...]
    ppermute x16, waiting for transfers between devices: 37 us -> 39.3 us  [swap(): return lax.ppermute(x, axis, [(i, i ^ distance) for i in range(size)])]
    ppermute x16, starting transfers between devices: 18.5 us -> 17 us  [swap(): return lax.ppermute(x, axis, [(i, i ^ distance) for i in range(size)])]
  transfers between devices with their start and end apart: 16 -> 16, of which waited for: 8 -> 8; matrix products, arithmetic and copies ran while one was open for 1% -> 1% of each run, Pallas kernels for 26% -> 25%
where the time goes in v4:
time: 94.5 us; the launch traced here: 94.4 us
  waiting for transfers between devices  39.3 us (42%)
  Pallas kernels  26.9 us (28%)
  starting transfers between devices  17 us (18%)
  local copies, waits for them, and re-layouts  8.37 us (9%)
  other arithmetic  1.73 us (2%)
    ppermute x16, waiting for transfers between devices, swap(): return lax.ppermute(x, axis, [(i, i ^ distance) for i in range(size)])  39.3 us
    ppermute x16, starting transfers between devices, swap(): return lax.ppermute(x, axis, [(i, i ^ distance) for i in range(size)])  17 us
    pallas_call x4, Pallas kernels, product_rows(): pl.pallas_call(product_body, in_specs=[pl.BlockSpec(memory_space=pltpu.SM...  11.6 us
    unnamed x20, local copies, waits for them, and re-layouts  8.26 us
    pallas_call x1, Pallas kernels, half_rows(): pl.pallas_call(functools.partial(half_body, blocks), in_specs=[smem] * 3...  6.91 us
    pallas_call x4, Pallas kernels, mix(): pl.pallas_call(functools.partial(mix_body, occ, which), in_specs=[pl.Bloc...  5.36 us
    pallas_call x1, Pallas kernels, window_rows(): pl.pallas_call(functools.partial(window_body, blocks, outs), in_specs=[sm...  2.95 us
  transfers between devices with their start and end apart: 16, of which 8 were waited for; matrix products, arithmetic and copies ran while one was open for 1% of the time, Pallas kernels for 25%

profile of v4, /device:TPU:0, one launch (start us, length us, event | category | flops | bytes accessed | tf_op | source)
XLA Modules:
  0.0 94.4 jit_solution(15922681155054834345)
XLA Ops:
  0.7 2.9 %shard_map.65 = (bf16[64,2048]{1,0:T(8,128)(2,1)}, bf16[64,2048]{1,0:T(8,128)(2,1)}) custom-call(s32[1,24]{1,0:T(1,128)} %rows.3, s32[1,24]{1,0:T(1,128)} %cols.3, s32[1,1]{1,0:T(1,128)S(6)} %copy.15.live, bf16[8,24,128,128]{3,2,1,0:T(8,128)(2,1)} %tiles.3, bf16[8192,256]{1,0:T(8,128)(2,1)} %orbitals.3), custom_call_target="tpu_custom_call" | custom-call | flops 1000000000 | bytes 3333333 | tf_op jit(solution)/shard_map/pallas_call | solution.py:72
  3.7 4.4 %collective-permute-start = (bf16[64,2048]{1,0:T(8,128)(2,1)}, bf16[64,2048]{1,0:T(8,128)(2,1)S(1)}, u32[]{:S(2)}, u32[]{:S(2)}) collective-permute-start(bf16[64,2048]{1,0:T(8,128)(2,1)} %get-tuple-element.18.near), channel_id=1, source_target_pairs={{0,8},{4,12},{8,0},{12,4},{1,9},{5,13},{9,1},{13,5},{2,10},{6,14},... | collective-permute-start | bytes 786440 | tf_op jit(solution)/shard_map/ppermute | solution.py:200
  8.5 2.8 %copy-done.1 = bf16[8,24,128,128]{3,2,1,0:T(8,128)(2,1)S(1)} copy-done((bf16[8,24,128,128]{3,2,1,0:T(8,128)(2,1)S(1)}, bf16[8,24,128,128]{3,2,1,0:T(8,128)(2,1)}, u32[]{:S(2)}) %copy-start.1) | copy-done | bytes 6291480
  11.3 2.2 %copy-done.2 = bf16[8192,256]{1,0:T(8,128)(2,1)S(1)} copy-done((bf16[8192,256]{1,0:T(8,128)(2,1)S(1)}, bf16[8192,256]{1,0:T(8,128)(2,1)}, u32[]{:S(2)}) %copy-start.2) | copy-done | bytes 4194328
  13.5 6.9 %shard_map.64 = (bf16[2048,2048]{1,0:T(8,128)(2,1)S(1)}, f32[2,8,16]{2,1,0:T(8,128)S(1)}) custom-call(s32[1,24]{1,0:T(1,128)S(1)} %copy-done.3, s32[1,24]{1,0:T(1,128)S(1)} %copy-done.4, s32[1,1]{1,0:T(1,128)S(6)} %copy.15.live, bf16[8,24,128,128]{3,2,1,0:T(8,128)(2,1)S(1)} %copy-done.1, bf16[8192,256]{1,0:T(8,128)(2,1)S(1)} %copy-done.2, ...), custom_call_target="tpu_custom_call" | custom-call | flops 20000000000 | bytes 66666664 | tf_op jit(solution)/shard_map/pallas_call | solution.py:118
  20.4 3.3 %copy-done.7 = bf16[2048,2048]{1,0:T(8,128)(2,1)} copy-done((bf16[2048,2048]{1,0:T(8,128)(2,1)}, bf16[2048,2048]{1,0:T(8,128)(2,1)S(1)}, u32[]{:S(2)}) %copy-start.7) | copy-done | bytes 8388632
  23.7 2.9 %collective-permute-done.far = bf16[64,2048]{1,0:T(8,128)(2,1)S(1)} collective-permute-done((bf16[64,2048]{1,0:T(8,128)(2,1)}, bf16[64,2048]{1,0:T(8,128)(2,1)S(1)}, u32[]{:S(2)}, u32[]{:S(2)}) %collective-permute-start) | collective-permute-done | bytes 262176 | tf_op jit(solution)/shard_map/ppermute | solution.py:200
  26.6 1.3 %shard_map.67 = bf16[64,2048]{1,0:T(8,128)(2,1)S(1)} custom-call(f32[2,8,16]{2,1,0:T(8,128)S(1)} %get-tuple-element.17.weight, bf16[64,2048]{1,0:T(8,128)(2,1)S(1)} %copy-done.6, bf16[64,2048]{1,0:T(8,128)(2,1)S(1)} %collective-permute-done.far), custom_call_target="tpu_custom_call" | custom-call | flops 2000000000 | bytes 6666666 | tf_op jit(solution)/shard_map/pallas_call | solution.py:155
  28.0 1.7 %collective-permute-start.1 = (bf16[64,2048]{1,0:T(8,128)(2,1)S(1)}, bf16[64,2048]{1,0:T(8,128)(2,1)S(1)}, u32[]{:S(2)}, u32[]{:S(2)}) collective-permute-start(bf16[64,2048]{1,0:T(8,128)(2,1)S(1)} %shard_map.67), channel_id=1, source_target_pairs={{0,4},{4,0},{8,12},{12,8},{1,5},{5,1},{9,13},{13,9},{2,6},{6,2},{1... | collective-permute-start | bytes 786440 | tf_op jit(solution)/shard_map/ppermute | solution.py:200
  29.7 1.5 %collective-permute-done.8.far = bf16[64,2048]{1,0:T(8,128)(2,1)S(1)} collective-permute-done((bf16[64,2048]{1,0:T(8,128)(2,1)}, bf16[64,2048]{1,0:T(8,128)(2,1)S(1)}, u32[]{:S(2)}, u32[]{:S(2)}) %collective-permute-start.8) | collective-permute-done | bytes 262176 | tf_op jit(solution)/shard_map/ppermute | solution.py:200
  37.4 1.5 %collective-permute-start.4 = (bf16[64,2048]{1,0:T(8,128)(2,1)S(1)}, bf16[64,2048]{1,0:T(8,128)(2,1)S(1)}, u32[]{:S(2)}, u32[]{:S(2)}) collective-permute-start(bf16[64,2048]{1,0:T(8,128)(2,1)S(1)} %add_convert_fusion.1.even), channel_id=1, source_target_pairs={{0,2},{1,3},{2,0},{3,1},{4,6},{5,7},{6,4},{7,5},{8,10},{9,11},{10,... | collective-permute-start | bytes 786440 | tf_op jit(solution)/shard_map/ppermute | solution.py:200
  38.9 3.5 %collective-permute-done.9 = bf16[64,2048]{1,0:T(8,128)(2,1)S(1)} collective-permute-done((bf16[64,2048]{1,0:T(8,128)(2,1)S(1)}, bf16[64,2048]{1,0:T(8,128)(2,1)S(1)}, u32[]{:S(2)}, u32[]{:S(2)}) %collective-permute-start.9) | collective-permute-done | bytes 262176 | tf_op jit(solution)/shard_map/ppermute | solution.py:200
  42.4 1.9 %collective-permute-start.12 = (bf16[64,2048]{1,0:T(8,128)(2,1)S(1)}, bf16[64,2048]{1,0:T(8,128)(2,1)S(1)}, u32[]{:S(2)}, u32[]{:S(2)}) collective-permute-start(bf16[64,2048]{1,0:T(8,128)(2,1)S(1)} %add_convert_fusion.even), channel_id=1, source_target_pairs={{0,2},{1,3},{2,0},{3,1},{4,6},{5,7},{6,4},{7,5},{8,10},{9,11},{10,... | collective-permute-start | bytes 786440 | tf_op jit(solution)/shard_map/ppermute | solution.py:200
  44.3 2.9 %shard_map.68 = (bf16[64,2048]{1,0:T(8,128)(2,1)S(1)}, f32[64,2048]{1,0:T(8,128)S(1)}) custom-call(s32[1]{0:T(128)} %bitcast.flag, bf16[64,2048]{1,0:T(8,128)(2,1)S(1)} %add_convert_fusion.1.even, bf16[64,2048]{1,0:T(8,128)(2,1)S(1)} %collective-permute-done.2.odd, bf16[2048,2048]{1,0:T(8,128)(2,1)S(1)} %bitcast.20), custom_call_target="tpu_custom_call" | custom-call | flops 3000000000 | bytes 10000000 | tf_op jit(solution)/shard_map/pallas_call | solution.py:184
  47.9 2.9 %shard_map.72 = (bf16[64,2048]{1,0:T(8,128)(2,1)S(1)}, f32[64,2048]{1,0:T(8,128)S(1)}) custom-call(s32[1]{0:T(128)} %bitcast.flag, bf16[64,2048]{1,0:T(8,128)(2,1)S(1)} %add_convert_fusion.even, bf16[64,2048]{1,0:T(8,128)(2,1)S(1)} %collective-permute-done.10.odd, bf16[2048,2048]{1,0:T(8,128)(2,1)S(1)} %bitcast.20), custom_call_target="tpu_custom_call" | custom-call | flops 3000000000 | bytes 10000000 | tf_op jit(solution)/shard_map/pallas_call | solution.py:184
  50.8 1.7 %collective-permute-start.11 = (bf16[64,2048]{1,0:T(8,128)(2,1)S(1)}, bf16[64,2048]{1,0:T(8,128)(2,1)S(1)}, u32[]{:S(2)}, u32[]{:S(2)}) collective-permute-start(bf16[64,2048]{1,0:T(8,128)(2,1)S(1)} %get-tuple-element.26), channel_id=1, source_target_pairs={{0,4},{4,0},{8,12},{12,8},{1,5},{5,1},{9,13},{13,9},{2,6},{6,2},{1... | collective-permute-start | bytes 786440 | tf_op jit(solution)/shard_map/ppermute | solution.py:200
  52.6 2.9 %shard_map.69 = (bf16[64,2048]{1,0:T(8,128)(2,1)S(1)}, f32[64,2048]{1,0:T(8,128)S(1)}) custom-call(s32[1]{0:T(128)} %bitcast.flag, bf16[64,2048]{1,0:T(8,128)(2,1)S(1)} %collective-permute-done.4.even, bf16[64,2048]{1,0:T(8,128)(2,1)S(1)} %collective-permute-done.5.odd, bf16[2048,2048]{1,0:T(8,128)(2,1)S(1)} %bitcast.20), custom_call_target="tpu_custom_call" | custom-call | flops 3000000000 | bytes 10000000 | tf_op jit(solution)/shard_map/pallas_call | solution.py:184
  55.9 2.9 %shard_map.73 = (bf16[64,2048]{1,0:T(8,128)(2,1)S(1)}, f32[64,2048]{1,0:T(8,128)S(1)}) custom-call(s32[1]{0:T(128)} %bitcast.flag, bf16[64,2048]{1,0:T(8,128)(2,1)S(1)} %collective-permute-done.12.even, bf16[64,2048]{1,0:T(8,128)(2,1)S(1)} %collective-permute-done.13.odd, bf16[2048,2048]{1,0:T(8,128)(2,1)S(1)} %bitcast.20), custom_call_target="tpu_custom_call" | custom-call | flops 3000000000 | bytes 10000000 | tf_op jit(solution)/shard_map/pallas_call | solution.py:184
  58.8 1.7 %collective-permute-start.14 = (bf16[64,2048]{1,0:T(8,128)(2,1)S(1)}, bf16[64,2048]{1,0:T(8,128)(2,1)S(1)}, u32[]{:S(2)}, u32[]{:S(2)}) collective-permute-start(bf16[64,2048]{1,0:T(8,128)(2,1)S(1)} %get-tuple-element.28), channel_id=1, source_target_pairs={{0,4},{4,0},{8,12},{12,8},{1,5},{5,1},{9,13},{13,9},{2,6},{6,2},{1... | collective-permute-start | bytes 786440 | tf_op jit(solution)/shard_map/ppermute | solution.py:200
  60.6 7.1 %collective-permute-done.6 = bf16[64,2048]{1,0:T(8,128)(2,1)S(1)} collective-permute-done((bf16[64,2048]{1,0:T(8,128)(2,1)S(1)}, bf16[64,2048]{1,0:T(8,128)(2,1)S(1)}, u32[]{:S(2)}, u32[]{:S(2)}) %collective-permute-start.6) | collective-permute-done | bytes 262176 | tf_op jit(solution)/shard_map/ppermute | solution.py:200
  67.8 2.0 %collective-permute-start.7 = (bf16[64,2048]{1,0:T(8,128)(2,1)S(1)}, bf16[64,2048]{1,0:T(8,128)(2,1)S(1)}, u32[]{:S(2)}, u32[]{:S(2)}) collective-permute-start(bf16[64,2048]{1,0:T(8,128)(2,1)S(1)} %select_convert_fusion.1), channel_id=1, source_target_pairs={{0,8},{4,12},{8,0},{12,4},{1,9},{5,13},{9,1},{13,5},{2,10},{6,14},... | collective-permute-start | bytes 786440 | tf_op jit(solution)/shard_map/ppermute | solution.py:200
  69.8 7.0 %collective-permute-done.14 = bf16[64,2048]{1,0:T(8,128)(2,1)S(1)} collective-permute-done((bf16[64,2048]{1,0:T(8,128)(2,1)S(1)}, bf16[64,2048]{1,0:T(8,128)(2,1)S(1)}, u32[]{:S(2)}, u32[]{:S(2)}) %collective-permute-start.14) | collective-permute-done | bytes 262176 | tf_op jit(solution)/shard_map/ppermute | solution.py:200
  76.9 12.3 %collective-permute-done.7 = bf16[64,2048]{1,0:T(8,128)(2,1)S(1)} collective-permute-done((bf16[64,2048]{1,0:T(8,128)(2,1)S(1)}, bf16[64,2048]{1,0:T(8,128)(2,1)S(1)}, u32[]{:S(2)}, u32[]{:S(2)}) %collective-permute-start.7) | collective-permute-done | bytes 262176 | tf_op jit(solution)/shard_map/ppermute | solution.py:200
  89.3 3.8 %collective-permute-done.15 = bf16[64,2048]{1,0:T(8,128)(2,1)S(1)} collective-permute-done((bf16[64,2048]{1,0:T(8,128)(2,1)S(1)}, bf16[64,2048]{1,0:T(8,128)(2,1)S(1)}, u32[]{:S(2)}, u32[]{:S(2)}) %collective-permute-start.15) | collective-permute-done | bytes 262176 | tf_op jit(solution)/shard_map/ppermute | solution.py:200
  (51 shorter events, 9.3 us)
Async XLA Ops:
  0.0 8.1 %copy-start = (bf16[32,32]{1,0:T(8,128)(2,1)S(1)}, bf16[32,32]{1,0:T(8,128)(2,1)}, u32[]{:S(2)}) copy-start(bf16[32,32]{1,0:T(8,128)(2,1)} %param.11) | copy-start | bytes 6148
  0.0 8.5 %copy-start.3 = (s32[1,24]{1,0:T(1,128)S(1)}, s32[1,24]{1,0:T(1,128)}, u32[]{:S(2)}) copy-start(s32[1,24]{1,0:T(1,128)} %rows.3) | copy-start | bytes 292
  0.0 8.5 %copy-start.4 = (s32[1,24]{1,0:T(1,128)S(1)}, s32[1,24]{1,0:T(1,128)}, u32[]{:S(2)}) copy-start(s32[1,24]{1,0:T(1,128)} %cols.3) | copy-start | bytes 292
  3.7 23.0 %collective-permute-start = (bf16[64,2048]{1,0:T(8,128)(2,1)}, bf16[64,2048]{1,0:T(8,128)(2,1)S(1)}, u32[]{:S(2)}, u32[]{:S(2)}) collective-permute-start(bf16[64,2048]{1,0:T(8,128)(2,1)} %get-tuple-element.18.near), channel_id=1, source_target_pairs={{0,8},{4,12},{8,0},{12,4},{1,9},{5,13},{9,1},{13,5},{2,10},{6,14},... | collective-permute-start | bytes 786440 | tf_op jit(solution)/shard_map/ppermute | solution.py:200
  8.0 23.2 %collective-permute-start.8 = (bf16[64,2048]{1,0:T(8,128)(2,1)}, bf16[64,2048]{1,0:T(8,128)(2,1)S(1)}, u32[]{:S(2)}, u32[]{:S(2)}) collective-permute-start(bf16[64,2048]{1,0:T(8,128)(2,1)} %get-tuple-element.24.near), channel_id=1, source_target_pairs={{0,8},{4,12},{8,0},{12,4},{1,9},{5,13},{9,1},{13,5},{2,10},{6,14},... | collective-permute-start | bytes 786440 | tf_op jit(solution)/shard_map/ppermute | solution.py:200
  13.5 13.1 %copy-start.6 = (bf16[64,2048]{1,0:T(8,128)(2,1)S(1)}, bf16[64,2048]{1,0:T(8,128)(2,1)}, u32[]{:S(2)}) copy-start(bf16[64,2048]{1,0:T(8,128)(2,1)} %get-tuple-element.18.near) | copy-start | bytes 786436
  20.4 3.3 %copy-start.7 = (bf16[2048,2048]{1,0:T(8,128)(2,1)}, bf16[2048,2048]{1,0:T(8,128)(2,1)S(1)}, u32[]{:S(2)}) copy-start(bf16[2048,2048]{1,0:T(8,128)(2,1)S(1)} %get-tuple-element.19.right) | copy-start | bytes 25165828
  23.7 7.5 %copy-start.5 = (bf16[64,2048]{1,0:T(8,128)(2,1)S(1)}, bf16[64,2048]{1,0:T(8,128)(2,1)}, u32[]{:S(2)}) copy-start(bf16[64,2048]{1,0:T(8,128)(2,1)} %get-tuple-element.24.near) | copy-start | bytes 786436
  28.0 9.3 %collective-permute-start.1 = (bf16[64,2048]{1,0:T(8,128)(2,1)S(1)}, bf16[64,2048]{1,0:T(8,128)(2,1)S(1)}, u32[]{:S(2)}, u32[]{:S(2)}) collective-permute-start(bf16[64,2048]{1,0:T(8,128)(2,1)S(1)} %shard_map.67), channel_id=1, source_target_pairs={{0,4},{4,0},{8,12},{12,8},{1,5},{5,1},{9,13},{13,9},{2,6},{6,2},{1... | collective-permute-start | bytes 786440 | tf_op jit(solution)/shard_map/ppermute | solution.py:200
  32.6 9.8 %collective-permute-start.9 = (bf16[64,2048]{1,0:T(8,128)(2,1)S(1)}, bf16[64,2048]{1,0:T(8,128)(2,1)S(1)}, u32[]{:S(2)}, u32[]{:S(2)}) collective-permute-start(bf16[64,2048]{1,0:T(8,128)(2,1)S(1)} %shard_map.71), channel_id=1, source_target_pairs={{0,4},{4,0},{8,12},{12,8},{1,5},{5,1},{9,13},{13,9},{2,6},{6,2},{1... | collective-permute-start | bytes 786440 | tf_op jit(solution)/shard_map/ppermute | solution.py:200
  33.4 10.9 %slice-start = ((s8[8388608]{0:T(1024)(128)(4,1)}), s8[4194304]{0:T(1024)(128)(4,1)S(1)}, s32[]{:S(2)}) async-start(s8[8388608]{0:T(1024)(128)(4,1)} %bitcast.19), calls=%async_computation | async-start | bytes 8388608
  34.7 9.6 %slice-start.1 = ((s8[8388608]{0:T(1024)(128)(4,1)}), s8[4194304]{0:T(1024)(128)(4,1)S(1)}, s32[]{:S(2)}) async-start(s8[8388608]{0:T(1024)(128)(4,1)} %bitcast.19), calls=%async_computation.1 | async-start | bytes 8388608
  37.4 10.0 %collective-permute-start.4 = (bf16[64,2048]{1,0:T(8,128)(2,1)S(1)}, bf16[64,2048]{1,0:T(8,128)(2,1)S(1)}, u32[]{:S(2)}, u32[]{:S(2)}) collective-permute-start(bf16[64,2048]{1,0:T(8,128)(2,1)S(1)} %add_convert_fusion.1.even), channel_id=1, source_target_pairs={{0,2},{1,3},{2,0},{3,1},{4,6},{5,7},{6,4},{7,5},{8,10},{9,11},{10,... | collective-permute-start | bytes 786440 | tf_op jit(solution)/shard_map/ppermute | solution.py:200
  38.9 5.5 %collective-permute-start.2 = (bf16[64,2048]{1,0:T(8,128)(2,1)S(1)}, bf16[64,2048]{1,0:T(8,128)(2,1)S(1)}, u32[]{:S(2)}, u32[]{:S(2)}) collective-permute-start(bf16[64,2048]{1,0:T(8,128)(2,1)S(1)} %add_convert_fusion.1.even), channel_id=1, source_target_pairs={{0,1},{1,0},{2,3},{3,2},{4,5},{5,4},{6,7},{7,6},{8,9},{9,8},{10,11... | collective-permute-start | bytes 786440 | tf_op jit(solution)/shard_map/ppermute | solution.py:200
  42.4 10.1 %collective-permute-start.12 = (bf16[64,2048]{1,0:T(8,128)(2,1)S(1)}, bf16[64,2048]{1,0:T(8,128)(2,1)S(1)}, u32[]{:S(2)}, u32[]{:S(2)}) collective-permute-start(bf16[64,2048]{1,0:T(8,128)(2,1)S(1)} %add_convert_fusion.even), channel_id=1, source_target_pairs={{0,2},{1,3},{2,0},{3,1},{4,6},{5,7},{6,4},{7,5},{8,10},{9,11},{10,... | collective-permute-start | bytes 786440 | tf_op jit(solution)/shard_map/ppermute | solution.py:200
  44.3 3.6 %collective-permute-start.10 = (bf16[64,2048]{1,0:T(8,128)(2,1)S(1)}, bf16[64,2048]{1,0:T(8,128)(2,1)S(1)}, u32[]{:S(2)}, u32[]{:S(2)}) collective-permute-start(bf16[64,2048]{1,0:T(8,128)(2,1)S(1)} %add_convert_fusion.even), channel_id=1, source_target_pairs={{0,1},{1,0},{2,3},{3,2},{4,5},{5,4},{6,7},{7,6},{8,9},{9,8},{10,11... | collective-permute-start | bytes 786440 | tf_op jit(solution)/shard_map/ppermute | solution.py:200
  47.3 13.3 %collective-permute-start.3 = (bf16[64,2048]{1,0:T(8,128)(2,1)S(1)}, bf16[64,2048]{1,0:T(8,128)(2,1)S(1)}, u32[]{:S(2)}, u32[]{:S(2)}) collective-permute-start(bf16[64,2048]{1,0:T(8,128)(2,1)S(1)} %get-tuple-element.21), channel_id=1, source_target_pairs={{0,4},{4,0},{8,12},{12,8},{1,5},{5,1},{9,13},{13,9},{2,6},{6,2},{1... | collective-permute-start | bytes 786440 | tf_op jit(solution)/shard_map/ppermute | solution.py:200
  47.3 5.2 %collective-permute-start.5 = (bf16[64,2048]{1,0:T(8,128)(2,1)S(1)}, bf16[64,2048]{1,0:T(8,128)(2,1)S(1)}, u32[]{:S(2)}, u32[]{:S(2)}) collective-permute-start(bf16[64,2048]{1,0:T(8,128)(2,1)S(1)} %collective-permute-done.4.even), channel_id=1, source_target_pairs={{0,1},{1,0},{2,3},{3,2},{4,5},{5,4},{6,7},{7,6},{8,9},{9,8},{10,11... | collective-permute-start | bytes 786440 | tf_op jit(solution)/shard_map/ppermute | solution.py:200
  50.8 18.9 %collective-permute-start.11 = (bf16[64,2048]{1,0:T(8,128)(2,1)S(1)}, bf16[64,2048]{1,0:T(8,128)(2,1)S(1)}, u32[]{:S(2)}, u32[]{:S(2)}) collective-permute-start(bf16[64,2048]{1,0:T(8,128)(2,1)S(1)} %get-tuple-element.26), channel_id=1, source_target_pairs={{0,4},{4,0},{8,12},{12,8},{1,5},{5,1},{9,13},{13,9},{2,6},{6,2},{1... | collective-permute-start | bytes 786440 | tf_op jit(solution)/shard_map/ppermute | solution.py:200
  52.5 3.4 %collective-permute-start.13 = (bf16[64,2048]{1,0:T(8,128)(2,1)S(1)}, bf16[64,2048]{1,0:T(8,128)(2,1)S(1)}, u32[]{:S(2)}, u32[]{:S(2)}) collective-permute-start(bf16[64,2048]{1,0:T(8,128)(2,1)S(1)} %collective-permute-done.12.even), channel_id=1, source_target_pairs={{0,1},{1,0},{2,3},{3,2},{4,5},{5,4},{6,7},{7,6},{8,9},{9,8},{10,11... | collective-permute-start | bytes 786440 | tf_op jit(solution)/shard_map/ppermute | solution.py:200
  55.5 12.2 %collective-permute-start.6 = (bf16[64,2048]{1,0:T(8,128)(2,1)S(1)}, bf16[64,2048]{1,0:T(8,128)(2,1)S(1)}, u32[]{:S(2)}, u32[]{:S(2)}) collective-permute-start(bf16[64,2048]{1,0:T(8,128)(2,1)S(1)} %get-tuple-element.23), channel_id=1, source_target_pairs={{0,4},{4,0},{8,12},{12,8},{1,5},{5,1},{9,13},{13,9},{2,6},{6,2},{1... | collective-permute-start | bytes 786440 | tf_op jit(solution)/shard_map/ppermute | solution.py:200
  58.8 17.9 %collective-permute-start.14 = (bf16[64,2048]{1,0:T(8,128)(2,1)S(1)}, bf16[64,2048]{1,0:T(8,128)(2,1)S(1)}, u32[]{:S(2)}, u32[]{:S(2)}) collective-permute-start(bf16[64,2048]{1,0:T(8,128)(2,1)S(1)} %get-tuple-element.28), channel_id=1, source_target_pairs={{0,4},{4,0},{8,12},{12,8},{1,5},{5,1},{9,13},{13,9},{2,6},{6,2},{1... | collective-permute-start | bytes 786440 | tf_op jit(solution)/shard_map/ppermute | solution.py:200
  67.8 21.4 %collective-permute-start.7 = (bf16[64,2048]{1,0:T(8,128)(2,1)S(1)}, bf16[64,2048]{1,0:T(8,128)(2,1)S(1)}, u32[]{:S(2)}, u32[]{:S(2)}) collective-permute-start(bf16[64,2048]{1,0:T(8,128)(2,1)S(1)} %select_convert_fusion.1), channel_id=1, source_target_pairs={{0,8},{4,12},{8,0},{12,4},{1,9},{5,13},{9,1},{13,5},{2,10},{6,14},... | collective-permute-start | bytes 786440 | tf_op jit(solution)/shard_map/ppermute | solution.py:200
  76.9 16.3 %collective-permute-start.15 = (bf16[64,2048]{1,0:T(8,128)(2,1)S(1)}, bf16[64,2048]{1,0:T(8,128)(2,1)S(1)}, u32[]{:S(2)}, u32[]{:S(2)}) collective-permute-start(bf16[64,2048]{1,0:T(8,128)(2,1)S(1)} %select_convert_fusion), channel_id=1, source_target_pairs={{0,8},{4,12},{8,0},{12,4},{1,9},{5,13},{9,1},{13,5},{2,10},{6,14},... | collective-permute-start | bytes 786440 | tf_op jit(solution)/shard_map/ppermute | solution.py:200
  (2 other events, 5.0 us)

commit v5 on v4

--- a/solution.py
+++ b/solution.py
@@ -8,8 +8,9 @@
 from jax.sharding import PartitionSpec as P
 
 KR = 128
-HALVES = 2
+HALVES = (48, 48, 32)
 LIMIT = 8 * 1024 * 1024
+MOST = 50 * 1024 * 1024
 WHOLE = 60 * 1024 * 1024
 F32 = jnp.float32
 BF16 = jnp.bfloat16
@@ -24,11 +25,13 @@
 def store_block(acc, outs, row, aux_dev):
     occ = acc.shape[1]
     width = acc.shape[0] // aux_dev
-    part = width // len(outs)
-    for k, out in enumerate(outs):
+    begin = 0
+    for out in outs:
+        part = min(out.shape[0], width)
         for q in range(aux_dev):
-            first = q * width + k * part
+            first = q * width + begin
             out[pl.ds(row, part), q * occ:(q + 1) * occ] = acc[first:first + part, :].astype(BF16)
+        begin += part
 
 
 def window_body(blocks, outs, rows, cols, live, tiles, orbitals, *rest):
@@ -40,8 +43,10 @@
         return (pltpu.make_async_copy(tiles.at[:, slot], tile.at[k], tile_sems.at[k]),
                 pltpu.make_async_copy(orbitals.at[pl.ds(row, width)], orb.at[k], orb_sems.at[k]))
 
+    count = jnp.max(live[...])
+
     def wanted(slot):
-        return (rows[0, slot] == 0) & (slot < live[0, 0])
+        return (rows[0, slot] == 0) & (slot < count)
 
     for copy in copies(0, 0):
         copy.start()
@@ -69,11 +74,12 @@
     blocks = basis // (width * lax.axis_size("row"))
     held = slots - blocks + 1
     smem, hbm = pl.BlockSpec(memory_space=pltpu.SMEM), pl.BlockSpec(memory_space=pltpu.HBM)
+    vmem = pl.BlockSpec(memory_space=pltpu.VMEM)
     return pl.pallas_call(
-        functools.partial(window_body, blocks, outs),
-        in_specs=[smem] * 3 + [hbm] * 2,
-        out_specs=[pl.BlockSpec(memory_space=pltpu.VMEM)] * outs,
-        out_shape=[jax.ShapeDtypeStruct((width // outs, aux_dev * occ), BF16)] * outs,
+        functools.partial(window_body, blocks, len(outs)),
+        in_specs=[smem, smem, vmem] + [hbm] * 2,
+        out_specs=[pl.BlockSpec(memory_space=pltpu.VMEM)] * len(outs),
+        out_shape=[jax.ShapeDtypeStruct((part, aux_dev * occ), BF16) for part in outs],
         scratch_shapes=[
             pltpu.VMEM((held, aux_dev, width, width), BF16),
             pltpu.VMEM((held, width, occ), BF16),
@@ -86,24 +92,45 @@
     )(rows, cols, live, tiles, orbitals)
 
 
-def half_body(blocks, rows, cols, live, tiles, orbitals, weights, out, same, acc):
+def half_body(blocks, rows, cols, live, tiles, orbitals, weights, out, same,
+              tile, orb, acc, tile_sems, orb_sems):
+    aux_dev, slots, width, _ = tiles.shape
+    occ = orbitals.shape[1]
+    count = jnp.minimum(jnp.max(live[...]), slots)
+
+    def copies(slot):
+        row = pl.multiple_of(cols[0, slot] * width, width)
+        return (pltpu.make_async_copy(tiles.at[:, slot], tile.at[slot], tile_sems.at[slot]),
+                pltpu.make_async_copy(orbitals.at[pl.ds(row, width)], orb.at[slot], orb_sems.at[slot]))
+
+    def start(slot, carry):
+        for copy in copies(slot):
+            copy.start()
+        return carry
+
+    def finish(slot):
+        for copy in copies(slot):
+            copy.wait()
+
+    lax.fori_loop(0, 4, start, 0)
+    lax.fori_loop(blocks, count, start, 0)
+    lax.fori_loop(4, blocks, start, 0)
     same[...] = weights[...]
-    aux_dev, slots, width, _ = tiles.shape
-
-    def columns(slot):
-        return orbitals[pl.ds(pl.multiple_of(cols[0, slot] * width, width), width), :]
 
     def block(b, carry):
-        add_slot(acc, tiles[:, b], columns(b), True)
+        finish(b)
+        add_slot(acc, tile[b], orb[b], True)
 
         def extra(slot, inner):
             @pl.when(rows[0, slot] == b)
             def _():
-                add_slot(acc, tiles[:, slot], columns(slot), False)
+                finish(slot)
+                add_slot(acc, tile[slot], orb[slot], False)
             return inner
 
-        lax.fori_loop(blocks, jnp.minimum(live[0, 0], slots), extra, 0)
-        store_block(acc, [out], pl.multiple_of(b * width, width), aux_dev)
+        lax.fori_loop(blocks, count, extra, 0)
+        row = pl.multiple_of(b * width, width)
+        store_block(acc, [out], row, aux_dev)
         return carry
 
     lax.fori_loop(0, blocks, block, 0)
@@ -114,17 +141,24 @@
     basis, occ = orbitals.shape
     blocks = basis // (width * lax.axis_size("row"))
     wide = aux_dev * occ
-    smem, vmem = pl.BlockSpec(memory_space=pltpu.SMEM), pl.BlockSpec(memory_space=pltpu.VMEM)
+    smem, hbm = pl.BlockSpec(memory_space=pltpu.SMEM), pl.BlockSpec(memory_space=pltpu.HBM)
+    vmem = pl.BlockSpec(memory_space=pltpu.VMEM)
     return pl.pallas_call(
         functools.partial(half_body, blocks),
-        in_specs=[smem] * 3 + [vmem] * 3,
+        in_specs=[smem, smem, vmem] + [hbm] * 2 + [vmem],
         out_specs=[vmem] * 2,
         out_shape=[
             jax.ShapeDtypeStruct((blocks * width, wide), BF16),
             jax.ShapeDtypeStruct(weights.shape, weights.dtype),
         ],
-        scratch_shapes=[pltpu.VMEM((aux_dev * width, occ), F32)],
-        compiler_params=pltpu.CompilerParams(vmem_limit_bytes=LIMIT),
+        scratch_shapes=[
+            pltpu.VMEM((slots, aux_dev, width, width), BF16),
+            pltpu.VMEM((slots, width, occ), BF16),
+            pltpu.VMEM((aux_dev * width, occ), F32),
+            pltpu.SemaphoreType.DMA((slots,)),
+            pltpu.SemaphoreType.DMA((slots,)),
+        ],
+        compiler_params=pltpu.CompilerParams(vmem_limit_bytes=MOST),
         cost_estimate=pl.CostEstimate(flops=20_000_000_000, bytes_accessed=66_666_666, transcendentals=0),
     )(rows, cols, live, tiles, orbitals, weights)
 
@@ -150,7 +184,7 @@
     lax.fori_loop(0, near.shape[0] // step, chunk, 0)
 
 
-def mix(weight, which, near, far, occ, dtype):
+def mix(weight, which, near, far, occ, dtype, flops):
     rows, wide = near.shape
     return pl.pallas_call(
         functools.partial(mix_body, occ, which),
@@ -158,11 +192,12 @@
         out_specs=pl.BlockSpec(memory_space=pltpu.VMEM),
         out_shape=jax.ShapeDtypeStruct((rows, wide), dtype),
         compiler_params=pltpu.CompilerParams(vmem_limit_bytes=LIMIT),
-        cost_estimate=pl.CostEstimate(flops=2_000_000_000, bytes_accessed=6_666_666, transcendentals=0),
+        cost_estimate=pl.CostEstimate(flops=flops, bytes_accessed=flops // 300, transcendentals=0),
     )(weight, near, far)
 
 
-def product_body(flag, even, odd, right, send, keep, left):
+def product_body(flag, even, odd, right, *rest):
+    sends, keep, left = rest[:-2], rest[-2], rest[-1]
     rows, count = even.shape[0], right.shape[0]
     step = 512
     for k, piece in ((0, even), (1, odd)):
@@ -173,26 +208,27 @@
         product = lax.dot_general(
             left[...], right[n * step:(n + 1) * step, :], (((1,), (1,)), ((), ())),
             preferred_element_type=F32)
-        send[:, n * step:(n + 1) * step] = product[:rows].astype(BF16)
+        part = count // len(sends)
+        send, first = sends[n * step // part], n * step % part
+        send[:, first:first + step] = product[:rows].astype(BF16)
         keep[:, n * step:(n + 1) * step] = product[rows:]
 
 
-def product_rows(flag, even, odd, right):
+def product_rows(flag, even, odd, right, parts, flops):
     rows, wide = even.shape
     count = right.shape[0]
     vmem = pl.BlockSpec(memory_space=pltpu.VMEM)
-    return pl.pallas_call(
+    *sends, keep = pl.pallas_call(
         product_body,
         in_specs=[pl.BlockSpec(memory_space=pltpu.SMEM)] + [vmem] * 3,
-        out_specs=[vmem] * 2,
+        out_specs=[vmem] * (parts + 1),
         scratch_shapes=[pltpu.VMEM((2 * rows, wide), BF16)],
-        out_shape=[
-            jax.ShapeDtypeStruct((rows, count), BF16),
-            jax.ShapeDtypeStruct((rows, count), F32),
-        ],
+        out_shape=[jax.ShapeDtypeStruct((rows, count // parts), BF16)] * parts + [
+            jax.ShapeDtypeStruct((rows, count), F32)],
         compiler_params=pltpu.CompilerParams(vmem_limit_bytes=LIMIT),
-        cost_estimate=pl.CostEstimate(flops=3_000_000_000, bytes_accessed=10_000_000, transcendentals=0),
+        cost_estimate=pl.CostEstimate(flops=flops, bytes_accessed=flops // 300, transcendentals=0),
     )(flag, even, odd, right)
+    return sends, keep
 
 
 def swap(x, axis, distance):
@@ -206,37 +242,40 @@
     table = squared.reshape(4, aux_dev, 4, aux_dev)
     pick = lambda p, q: table[p, :, q, :]
     weights = jnp.stack([jnp.concatenate([pick(p, z), pick(p, z ^ 2)], axis=1) for p in (z ^ 1, z)])
-    window = window_rows(*args, HALVES)
     flag = jnp.reshape((r ^ z) & 1, (1,))
     first_own = ((r ^ z) & 2) == 0
+    window = window_rows(*args, HALVES)
+    right, weights = half_rows(*args, weights)
     fars = [swap(x, "aux", 2) for x in window]
-    right, weights = half_rows(*args, weights)
-    pieces, sums, ready = [], [[], []], None
+    pieces, sums = [], []
     for x, far in zip(window, fars):
-        message = swap(mix(weights, 0, x, far, occ, BF16), "aux", 1)
-        mine = mix(weights, 1, x, far, occ, F32)
+        message = swap(mix(weights, 0, x, far, occ, BF16, 2_000_000_000), "aux", 1)
+        mine = mix(weights, 1, x, far, occ, F32, 2_000_000_000)
         g0 = (mine + message.astype(F32)).astype(BF16)
         g1 = swap(g0, "row", 1)
         pieces.append(swap(g0, "row", 2))
-        send, ready = product_rows(flag, g0, g1, right)
-        sums[0].append(ready)
-        sums[1].append(swap(send, "aux", 1))
-    sums[0] = [keep + came.astype(F32) for keep, came in zip(*sums)]
-    sums[1] = []
-    for g2 in pieces:
-        send, keep = product_rows(flag, g2, swap(g2, "row", 1), right)
-        sums[1].append(keep + swap(send, "aux", 1).astype(F32))
+        sends, keep = product_rows(flag, g0, g1, right, 1, 3_000_000_000)
+        got = [swap(send, "aux", 1).astype(F32) for send in sends]
+        sums.append([keep + (got[0] if len(got) == 1 else jnp.concatenate(got, axis=1))])
+    for g2, total, parts in zip(pieces, sums, (1,) * len(sums)):
+        sends, keep = product_rows(flag, g2, swap(g2, "row", 1), right, parts, 3_000_000_000)
+        total.append((keep, [swap(send, "aux", 1) for send in sends]))
     results = []
-    for early, late in zip(*sums):
-        passed = swap(jnp.where(first_own, late, early).astype(BF16), "aux", 2)
-        results.append(jnp.where(first_own, early, late) + passed.astype(F32))
+    for early, (keep, came) in sums:
+        parts, step = [], keep.shape[1] // len(came)
+        for k, got in enumerate(came):
+            span = slice(k * step, (k + 1) * step)
+            late = keep[:, span] + got.astype(F32)
+            passed = swap(jnp.where(first_own, late, early[:, span]).astype(BF16), "aux", 2)
+            parts.append(jnp.where(first_own, early[:, span], late) + passed.astype(F32))
+        results.append(parts[0] if len(parts) == 1 else jnp.concatenate(parts, axis=1))
     return jnp.concatenate(results, axis=0)
 
 
 def any_mesh(args, squared):
     aux_dev, occ = args[0].shape[0], args[-1].shape[1]
-    window, = window_rows(*args, 1)
     right, squared = half_rows(*args, squared)
+    window = right[:KR]
     rows = window.shape[0]
     aux = lax.axis_size("aux")
     gathered = lax.all_gather(window, "aux", axis=0, tiled=True).reshape(aux, rows, aux_dev, occ)

time: 94.5 us -> 90.9 us (0.962)
  waiting for transfers between devices: 39.3 us -> 20.9 us
  starting transfers between devices: 17 us -> 29.8 us
  Pallas kernels: 26.9 us -> 36.7 us
  local copies, waits for them, and re-layouts: 8.37 us -> 0.15 us
    ppermute x16 -> x24, waiting for transfers between devices: 39.3 us -> 20.9 us  [swap(): return lax.ppermute(x, axis, [(i, i ^ distance) for i in range(size)])]
    ppermute x16 -> x24, starting transfers between devices: 17 us -> 29.8 us  [swap(): return lax.ppermute(x, axis, [(i, i ^ distance) for i in range(size)])]
    unnamed x20 -> x16, local copies, waits for them, and re-layouts: 8.26 us -> 0.04 us
    pallas_call x4 -> x6, Pallas kernels: 11.6 us -> 16 us  [product_rows(): pl.pallas_call(product_body, in_specs=[pl.BlockSpec(memory_space=pltpu.SM...]
    pallas_call x2, Pallas kernels: 9.86 us -> 13.8 us  [the longest x1 10.9 us: half_rows(): pl.pallas_call(functools.partial(half_body, blocks), in_specs=[smem, smem...]
    pallas_call x4 -> x6, Pallas kernels: 5.36 us -> 6.88 us  [mix(): pl.pallas_call(functools.partial(mix_body, occ, which), in_specs=[pl.Bloc...]
  transfers between devices with their start and end apart: 16 -> 24, of which waited for: 8 -> 7; matrix products, arithmetic and copies ran while one was open for 1% -> 1% of each run, Pallas kernels for 25% -> 37%
where the time goes in v5:
time: 90.9 us; the launch traced here: 90.5 us
  Pallas kernels  36.7 us (40%)
  starting transfers between devices  29.8 us (33%)
  waiting for transfers between devices  20.9 us (23%)
  other arithmetic  1.74 us (2%)
  between operations  1.02 us (1%)
    ppermute x24, starting transfers between devices, swap(): return lax.ppermute(x, axis, [(i, i ^ distance) for i in range(size)])  29.8 us
    ppermute x24, waiting for transfers between devices, swap(): return lax.ppermute(x, axis, [(i, i ^ distance) for i in range(size)])  20.9 us
    pallas_call x6, Pallas kernels, product_rows(): pl.pallas_call(product_body, in_specs=[pl.BlockSpec(memory_space=pltpu.SM...  16 us
    pallas_call x1, Pallas kernels, half_rows(): pl.pallas_call(functools.partial(half_body, blocks), in_specs=[smem, smem...  10.9 us
    pallas_call x6, Pallas kernels, mix(): pl.pallas_call(functools.partial(mix_body, occ, which), in_specs=[pl.Bloc...  6.88 us
    pallas_call x1, Pallas kernels, window_rows(): pl.pallas_call(functools.partial(window_body, blocks, len(outs)), in_spec...  2.93 us
  transfers between devices with their start and end apart: 24, of which 7 were waited for; matrix products, arithmetic and copies ran while one was open for 1% of the time, Pallas kernels for 37%

profile of v5, /device:TPU:0, one launch (start us, length us, event | category | flops | bytes accessed | tf_op | source)
XLA Modules:
  0.0 90.5 jit_solution(3135565881817464970)
XLA Ops:
  0.7 2.9 %shard_map.65 = (bf16[48,2048]{1,0:T(8,128)(2,1)}, bf16[48,2048]{1,0:T(8,128)(2,1)}, bf16[32,2048]{1,0:T(8,128)(2,1)}) custom-call(s32[1,24]{1,0:T(1,128)} %rows.3, s32[1,24]{1,0:T(1,128)} %cols.3, s32[1,1]{1,0:T(1,128)S(6)} %copy.15.live, bf16[8,24,128,128]{3,2,1,0:T(8,128)(2,1)} %tiles.3, bf16[8192,256]{1,0:T(8,128)(2,1)} %orbitals.3), custom_call_target="tpu_custom_call" | custom-call | flops 1000000000 | bytes 3333333 | tf_op jit(solution)/shard_map/pallas_call | solution.py:78
  3.6 4.1 %collective-permute-start.16 = (bf16[32,2048]{1,0:T(8,128)(2,1)}, bf16[32,2048]{1,0:T(8,128)(2,1)S(1)}, u32[]{:S(2)}, u32[]{:S(2)}) collective-permute-start(bf16[32,2048]{1,0:T(8,128)(2,1)} %get-tuple-element.34.near), channel_id=1, source_target_pairs={{0,8},{4,12},{8,0},{12,4},{1,9},{5,13},{9,1},{13,5},{2,10},{6,14},... | collective-permute-start | bytes 393224 | tf_op jit(solution)/shard_map/ppermute | solution.py:236
  7.8 2.8 %collective-permute-start = (bf16[48,2048]{1,0:T(8,128)(2,1)}, bf16[48,2048]{1,0:T(8,128)(2,1)S(1)}, u32[]{:S(2)}, u32[]{:S(2)}) collective-permute-start(bf16[48,2048]{1,0:T(8,128)(2,1)} %get-tuple-element.23.near), channel_id=1, source_target_pairs={{0,8},{4,12},{8,0},{12,4},{1,9},{5,13},{9,1},{13,5},{2,10},{6,14},... | collective-permute-start | bytes 589832 | tf_op jit(solution)/shard_map/ppermute | solution.py:236
  11.1 10.9 %shard_map.64 = (bf16[2048,2048]{1,0:T(8,128)(2,1)}, f32[2,8,16]{2,1,0:T(8,128)S(1)}) custom-call(s32[1,24]{1,0:T(1,128)S(1)} %copy-done.1, s32[1,24]{1,0:T(1,128)S(1)} %copy-done.2, s32[1,1]{1,0:T(1,128)S(6)} %copy.15.live, bf16[8,24,128,128]{3,2,1,0:T(8,128)(2,1)} %tiles.3, bf16[8192,256]{1,0:T(8,128)(2,1)} %orbitals.3, ...), custom_call_target="tpu_custom_call" | custom-call | flops 20000000000 | bytes 66666664 | tf_op jit(solution)/shard_map/pallas_call | solution.py:146
  22.0 1.5 %collective-permute-done.16.far = bf16[32,2048]{1,0:T(8,128)(2,1)S(1)} collective-permute-done((bf16[32,2048]{1,0:T(8,128)(2,1)}, bf16[32,2048]{1,0:T(8,128)(2,1)S(1)}, u32[]{:S(2)}, u32[]{:S(2)}) %collective-permute-start.16) | collective-permute-done | bytes 131104 | tf_op jit(solution)/shard_map/ppermute | solution.py:236
  24.5 3.5 %collective-permute-start.17 = (bf16[32,2048]{1,0:T(8,128)(2,1)S(1)}, bf16[32,2048]{1,0:T(8,128)(2,1)S(1)}, u32[]{:S(2)}, u32[]{:S(2)}) collective-permute-start(bf16[32,2048]{1,0:T(8,128)(2,1)S(1)} %shard_map.75), channel_id=1, source_target_pairs={{0,4},{4,0},{8,12},{12,8},{1,5},{5,1},{9,13},{13,9},{2,6},{6,2},{1... | collective-permute-start | bytes 393224 | tf_op jit(solution)/shard_map/ppermute | solution.py:236
  29.1 1.2 %shard_map.71 = bf16[48,2048]{1,0:T(8,128)(2,1)S(1)} custom-call(f32[2,8,16]{2,1,0:T(8,128)S(1)} %get-tuple-element.22.weight, bf16[48,2048]{1,0:T(8,128)(2,1)S(1)} %copy-done.4, bf16[48,2048]{1,0:T(8,128)(2,1)S(1)} %collective-permute-done.8.far), custom_call_target="tpu_custom_call" | custom-call | flops 2000000000 | bytes 6666666 | tf_op jit(solution)/shard_map/pallas_call | solution.py:189
  32.4 1.2 %collective-permute-start.1 = (bf16[48,2048]{1,0:T(8,128)(2,1)S(1)}, bf16[48,2048]{1,0:T(8,128)(2,1)S(1)}, u32[]{:S(2)}, u32[]{:S(2)}) collective-permute-start(bf16[48,2048]{1,0:T(8,128)(2,1)S(1)} %shard_map.67), channel_id=1, source_target_pairs={{0,4},{4,0},{8,12},{12,8},{1,5},{5,1},{9,13},{13,9},{2,6},{6,2},{1... | collective-permute-start | bytes 589832 | tf_op jit(solution)/shard_map/ppermute | solution.py:236
  34.9 1.4 %shard_map.66 = f32[48,2048]{1,0:T(8,128)S(1)} custom-call(f32[2,8,16]{2,1,0:T(8,128)S(1)} %get-tuple-element.22.weight, bf16[48,2048]{1,0:T(8,128)(2,1)S(1)} %copy-done.3, bf16[48,2048]{1,0:T(8,128)(2,1)S(1)} %collective-permute-done.far), custom_call_target="tpu_custom_call" | custom-call | flops 2000000000 | bytes 6666666 | tf_op jit(solution)/shard_map/pallas_call | solution.py:189
  36.3 1.2 %collective-permute-start.20 = (bf16[32,2048]{1,0:T(8,128)(2,1)S(1)}, bf16[32,2048]{1,0:T(8,128)(2,1)S(1)}, u32[]{:S(2)}, u32[]{:S(2)}) collective-permute-start(bf16[32,2048]{1,0:T(8,128)(2,1)S(1)} %add_convert_fusion.2.even), channel_id=1, source_target_pairs={{0,2},{1,3},{2,0},{3,1},{4,6},{5,7},{6,4},{7,5},{8,10},{9,11},{10,... | collective-permute-start | bytes 393224 | tf_op jit(solution)/shard_map/ppermute | solution.py:236
  37.5 2.7 %shard_map.76 = (bf16[32,2048]{1,0:T(8,128)(2,1)S(1)}, f32[32,2048]{1,0:T(8,128)S(1)}) custom-call(s32[1]{0:T(128)} %bitcast.flag, bf16[32,2048]{1,0:T(8,128)(2,1)S(1)} %add_convert_fusion.2.even, bf16[32,2048]{1,0:T(8,128)(2,1)S(1)} %collective-permute-done.18.odd, bf16[2048,2048]{1,0:T(8,128)(2,1)S(1)} %bitcast.20), custom_call_target="tpu_custom_call" | custom-call | flops 3000000000 | bytes 10000000 | tf_op jit(solution)/shard_map/pallas_call | solution.py:221
  40.1 1.4 %collective-permute-start.19 = (bf16[32,2048]{1,0:T(8,128)(2,1)S(1)}, bf16[32,2048]{1,0:T(8,128)(2,1)S(1)}, u32[]{:S(2)}, u32[]{:S(2)}) collective-permute-start(bf16[32,2048]{1,0:T(8,128)(2,1)S(1)} %get-tuple-element.36), channel_id=1, source_target_pairs={{0,4},{4,0},{8,12},{12,8},{1,5},{5,1},{9,13},{13,9},{2,6},{6,2},{1... | collective-permute-start | bytes 393224 | tf_op jit(solution)/shard_map/ppermute | solution.py:236
  45.1 2.7 %shard_map.77 = (bf16[32,2048]{1,0:T(8,128)(2,1)S(1)}, f32[32,2048]{1,0:T(8,128)S(1)}) custom-call(s32[1]{0:T(128)} %bitcast.flag, bf16[32,2048]{1,0:T(8,128)(2,1)S(1)} %collective-permute-done.20.even, bf16[32,2048]{1,0:T(8,128)(2,1)S(1)} %collective-permute-done.21.odd, bf16[2048,2048]{1,0:T(8,128)(2,1)S(1)} %bitcast.20), custom_call_target="tpu_custom_call" | custom-call | flops 3000000000 | bytes 10000000 | tf_op jit(solution)/shard_map/pallas_call | solution.py:221
  48.8 2.7 %shard_map.72 = (bf16[48,2048]{1,0:T(8,128)(2,1)S(1)}, f32[48,2048]{1,0:T(8,128)S(1)}) custom-call(s32[1]{0:T(128)} %bitcast.flag, bf16[48,2048]{1,0:T(8,128)(2,1)S(1)} %add_convert_fusion.even, bf16[48,2048]{1,0:T(8,128)(2,1)S(1)} %collective-permute-done.10.odd, bf16[2048,2048]{1,0:T(8,128)(2,1)S(1)} %bitcast.20), custom_call_target="tpu_custom_call" | custom-call | flops 3000000000 | bytes 10000000 | tf_op jit(solution)/shard_map/pallas_call | solution.py:221
  52.6 2.7 %shard_map.68 = (bf16[48,2048]{1,0:T(8,128)(2,1)S(1)}, f32[48,2048]{1,0:T(8,128)S(1)}) custom-call(s32[1]{0:T(128)} %bitcast.flag, bf16[48,2048]{1,0:T(8,128)(2,1)S(1)} %add_convert_fusion.1.even, bf16[48,2048]{1,0:T(8,128)(2,1)S(1)} %collective-permute-done.2.odd, bf16[2048,2048]{1,0:T(8,128)(2,1)S(1)} %bitcast.20), custom_call_target="tpu_custom_call" | custom-call | flops 3000000000 | bytes 10000000 | tf_op jit(solution)/shard_map/pallas_call | solution.py:221
  56.9 2.4 %collective-permute-start.23 = (bf16[32,2048]{1,0:T(8,128)(2,1)S(1)}, bf16[32,2048]{1,0:T(8,128)(2,1)S(1)}, u32[]{:S(2)}, u32[]{:S(2)}) collective-permute-start(bf16[32,2048]{1,0:T(8,128)(2,1)S(1)} %select_convert_fusion.2), channel_id=1, source_target_pairs={{0,8},{4,12},{8,0},{12,4},{1,9},{5,13},{9,1},{13,5},{2,10},{6,14},... | collective-permute-start | bytes 393224 | tf_op jit(solution)/shard_map/ppermute | solution.py:236
  59.3 2.7 %shard_map.73 = (bf16[48,2048]{1,0:T(8,128)(2,1)S(1)}, f32[48,2048]{1,0:T(8,128)S(1)}) custom-call(s32[1]{0:T(128)} %bitcast.flag, bf16[48,2048]{1,0:T(8,128)(2,1)S(1)} %collective-permute-done.12.even, bf16[48,2048]{1,0:T(8,128)(2,1)S(1)} %collective-permute-done.13.odd, bf16[2048,2048]{1,0:T(8,128)(2,1)S(1)} %bitcast.20), custom_call_target="tpu_custom_call" | custom-call | flops 3000000000 | bytes 10000000 | tf_op jit(solution)/shard_map/pallas_call | solution.py:221
  62.0 1.7 %collective-permute-start.14 = (bf16[48,2048]{1,0:T(8,128)(2,1)S(1)}, bf16[48,2048]{1,0:T(8,128)(2,1)S(1)}, u32[]{:S(2)}, u32[]{:S(2)}) collective-permute-start(bf16[48,2048]{1,0:T(8,128)(2,1)S(1)} %get-tuple-element.33), channel_id=1, source_target_pairs={{0,4},{4,0},{8,12},{12,8},{1,5},{5,1},{9,13},{13,9},{2,6},{6,2},{1... | collective-permute-start | bytes 589832 | tf_op jit(solution)/shard_map/ppermute | solution.py:236
  63.7 2.7 %shard_map.69 = (bf16[48,2048]{1,0:T(8,128)(2,1)S(1)}, f32[48,2048]{1,0:T(8,128)S(1)}) custom-call(s32[1]{0:T(128)} %bitcast.flag, bf16[48,2048]{1,0:T(8,128)(2,1)S(1)} %collective-permute-done.4.even, bf16[48,2048]{1,0:T(8,128)(2,1)S(1)} %collective-permute-done.5.odd, bf16[2048,2048]{1,0:T(8,128)(2,1)S(1)} %bitcast.20), custom_call_target="tpu_custom_call" | custom-call | flops 3000000000 | bytes 10000000 | tf_op jit(solution)/shard_map/pallas_call | solution.py:221
  66.9 3.1 %collective-permute-done.14 = bf16[48,2048]{1,0:T(8,128)(2,1)S(1)} collective-permute-done((bf16[48,2048]{1,0:T(8,128)(2,1)S(1)}, bf16[48,2048]{1,0:T(8,128)(2,1)S(1)}, u32[]{:S(2)}, u32[]{:S(2)}) %collective-permute-start.14) | collective-permute-done | bytes 196640 | tf_op jit(solution)/shard_map/ppermute | solution.py:236
  70.1 3.2 %collective-permute-start.15 = (bf16[48,2048]{1,0:T(8,128)(2,1)S(1)}, bf16[48,2048]{1,0:T(8,128)(2,1)S(1)}, u32[]{:S(2)}, u32[]{:S(2)}) collective-permute-start(bf16[48,2048]{1,0:T(8,128)(2,1)S(1)} %select_convert_fusion), channel_id=1, source_target_pairs={{0,8},{4,12},{8,0},{12,4},{1,9},{5,13},{9,1},{13,5},{2,10},{6,14},... | collective-permute-start | bytes 589832 | tf_op jit(solution)/shard_map/ppermute | solution.py:236
  73.3 3.0 %collective-permute-done.6 = bf16[48,2048]{1,0:T(8,128)(2,1)S(1)} collective-permute-done((bf16[48,2048]{1,0:T(8,128)(2,1)S(1)}, bf16[48,2048]{1,0:T(8,128)(2,1)S(1)}, u32[]{:S(2)}, u32[]{:S(2)}) %collective-permute-start.6) | collective-permute-done | bytes 196640 | tf_op jit(solution)/shard_map/ppermute | solution.py:236
  77.5 8.7 %collective-permute-done.15 = bf16[48,2048]{1,0:T(8,128)(2,1)S(1)} collective-permute-done((bf16[48,2048]{1,0:T(8,128)(2,1)S(1)}, bf16[48,2048]{1,0:T(8,128)(2,1)S(1)}, u32[]{:S(2)}, u32[]{:S(2)}) %collective-permute-start.15) | collective-permute-done | bytes 196640 | tf_op jit(solution)/shard_map/ppermute | solution.py:236
  86.3 3.0 %collective-permute-done.7 = bf16[48,2048]{1,0:T(8,128)(2,1)S(1)} collective-permute-done((bf16[48,2048]{1,0:T(8,128)(2,1)S(1)}, bf16[48,2048]{1,0:T(8,128)(2,1)S(1)}, u32[]{:S(2)}, u32[]{:S(2)}) %collective-permute-start.7) | collective-permute-done | bytes 196640 | tf_op jit(solution)/shard_map/ppermute | solution.py:236
  (70 shorter events, 16.3 us)
Async XLA Ops:
  3.6 19.9 %collective-permute-start.16 = (bf16[32,2048]{1,0:T(8,128)(2,1)}, bf16[32,2048]{1,0:T(8,128)(2,1)S(1)}, u32[]{:S(2)}, u32[]{:S(2)}) collective-permute-start(bf16[32,2048]{1,0:T(8,128)(2,1)} %get-tuple-element.34.near), channel_id=1, source_target_pairs={{0,8},{4,12},{8,0},{12,4},{1,9},{5,13},{9,1},{13,5},{2,10},{6,14},... | collective-permute-start | bytes 393224 | tf_op jit(solution)/shard_map/ppermute | solution.py:236
  7.7 21.3 %collective-permute-start.8 = (bf16[48,2048]{1,0:T(8,128)(2,1)}, bf16[48,2048]{1,0:T(8,128)(2,1)S(1)}, u32[]{:S(2)}, u32[]{:S(2)}) collective-permute-start(bf16[48,2048]{1,0:T(8,128)(2,1)} %get-tuple-element.29.near), channel_id=1, source_target_pairs={{0,8},{4,12},{8,0},{12,4},{1,9},{5,13},{9,1},{13,5},{2,10},{6,14},... | collective-permute-start | bytes 589832 | tf_op jit(solution)/shard_map/ppermute | solution.py:236
  7.8 23.4 %collective-permute-start = (bf16[48,2048]{1,0:T(8,128)(2,1)}, bf16[48,2048]{1,0:T(8,128)(2,1)S(1)}, u32[]{:S(2)}, u32[]{:S(2)}) collective-permute-start(bf16[48,2048]{1,0:T(8,128)(2,1)} %get-tuple-element.23.near), channel_id=1, source_target_pairs={{0,8},{4,12},{8,0},{12,4},{1,9},{5,13},{9,1},{13,5},{2,10},{6,14},... | collective-permute-start | bytes 589832 | tf_op jit(solution)/shard_map/ppermute | solution.py:236
  24.5 10.3 %collective-permute-start.17 = (bf16[32,2048]{1,0:T(8,128)(2,1)S(1)}, bf16[32,2048]{1,0:T(8,128)(2,1)S(1)}, u32[]{:S(2)}, u32[]{:S(2)}) collective-permute-start(bf16[32,2048]{1,0:T(8,128)(2,1)S(1)} %shard_map.75), channel_id=1, source_target_pairs={{0,4},{4,0},{8,12},{12,8},{1,5},{5,1},{9,13},{13,9},{2,6},{6,2},{1... | collective-permute-start | bytes 393224 | tf_op jit(solution)/shard_map/ppermute | solution.py:236
  30.2 12.0 %collective-permute-start.9 = (bf16[48,2048]{1,0:T(8,128)(2,1)S(1)}, bf16[48,2048]{1,0:T(8,128)(2,1)S(1)}, u32[]{:S(2)}, u32[]{:S(2)}) collective-permute-start(bf16[48,2048]{1,0:T(8,128)(2,1)S(1)} %shard_map.71), channel_id=1, source_target_pairs={{0,4},{4,0},{8,12},{12,8},{1,5},{5,1},{9,13},{13,9},{2,6},{6,2},{1... | collective-permute-start | bytes 589832 | tf_op jit(solution)/shard_map/ppermute | solution.py:236
  32.4 11.6 %collective-permute-start.1 = (bf16[48,2048]{1,0:T(8,128)(2,1)S(1)}, bf16[48,2048]{1,0:T(8,128)(2,1)S(1)}, u32[]{:S(2)}, u32[]{:S(2)}) collective-permute-start(bf16[48,2048]{1,0:T(8,128)(2,1)S(1)} %shard_map.67), channel_id=1, source_target_pairs={{0,4},{4,0},{8,12},{12,8},{1,5},{5,1},{9,13},{13,9},{2,6},{6,2},{1... | collective-permute-start | bytes 589832 | tf_op jit(solution)/shard_map/ppermute | solution.py:236
  34.8 2.6 %collective-permute-start.18 = (bf16[32,2048]{1,0:T(8,128)(2,1)S(1)}, bf16[32,2048]{1,0:T(8,128)(2,1)S(1)}, u32[]{:S(2)}, u32[]{:S(2)}) collective-permute-start(bf16[32,2048]{1,0:T(8,128)(2,1)S(1)} %add_convert_fusion.2.even), channel_id=1, source_target_pairs={{0,1},{1,0},{2,3},{3,2},{4,5},{5,4},{6,7},{7,6},{8,9},{9,8},{10,11... | collective-permute-start | bytes 393224 | tf_op jit(solution)/shard_map/ppermute | solution.py:236
  36.3 6.0 %collective-permute-start.20 = (bf16[32,2048]{1,0:T(8,128)(2,1)S(1)}, bf16[32,2048]{1,0:T(8,128)(2,1)S(1)}, u32[]{:S(2)}, u32[]{:S(2)}) collective-permute-start(bf16[32,2048]{1,0:T(8,128)(2,1)S(1)} %add_convert_fusion.2.even), channel_id=1, source_target_pairs={{0,2},{1,3},{2,0},{3,1},{4,6},{5,7},{6,4},{7,5},{8,10},{9,11},{10,... | collective-permute-start | bytes 393224 | tf_op jit(solution)/shard_map/ppermute | solution.py:236
  40.1 15.1 %collective-permute-start.19 = (bf16[32,2048]{1,0:T(8,128)(2,1)S(1)}, bf16[32,2048]{1,0:T(8,128)(2,1)S(1)}, u32[]{:S(2)}, u32[]{:S(2)}) collective-permute-start(bf16[32,2048]{1,0:T(8,128)(2,1)S(1)} %get-tuple-element.36), channel_id=1, source_target_pairs={{0,4},{4,0},{8,12},{12,8},{1,5},{5,1},{9,13},{13,9},{2,6},{6,2},{1... | collective-permute-start | bytes 393224 | tf_op jit(solution)/shard_map/ppermute | solution.py:236
  42.2 1.9 %collective-permute-start.21 = (bf16[32,2048]{1,0:T(8,128)(2,1)S(1)}, bf16[32,2048]{1,0:T(8,128)(2,1)S(1)}, u32[]{:S(2)}, u32[]{:S(2)}) collective-permute-start(bf16[32,2048]{1,0:T(8,128)(2,1)S(1)} %collective-permute-done.20.even), channel_id=1, source_target_pairs={{0,1},{1,0},{2,3},{3,2},{4,5},{5,4},{6,7},{7,6},{8,9},{9,8},{10,11... | collective-permute-start | bytes 393224 | tf_op jit(solution)/shard_map/ppermute | solution.py:236
  42.3 5.5 %collective-permute-start.10 = (bf16[48,2048]{1,0:T(8,128)(2,1)S(1)}, bf16[48,2048]{1,0:T(8,128)(2,1)S(1)}, u32[]{:S(2)}, u32[]{:S(2)}) collective-permute-start(bf16[48,2048]{1,0:T(8,128)(2,1)S(1)} %add_convert_fusion.even), channel_id=1, source_target_pairs={{0,1},{1,0},{2,3},{3,2},{4,5},{5,4},{6,7},{7,6},{8,9},{9,8},{10,11... | collective-permute-start | bytes 589832 | tf_op jit(solution)/shard_map/ppermute | solution.py:236
  42.9 13.5 %collective-permute-start.12 = (bf16[48,2048]{1,0:T(8,128)(2,1)S(1)}, bf16[48,2048]{1,0:T(8,128)(2,1)S(1)}, u32[]{:S(2)}, u32[]{:S(2)}) collective-permute-start(bf16[48,2048]{1,0:T(8,128)(2,1)S(1)} %add_convert_fusion.even), channel_id=1, source_target_pairs={{0,2},{1,3},{2,0},{3,1},{4,6},{5,7},{6,4},{7,5},{8,10},{9,11},{10,... | collective-permute-start | bytes 589832 | tf_op jit(solution)/shard_map/ppermute | solution.py:236
  44.0 7.5 %collective-permute-start.2 = (bf16[48,2048]{1,0:T(8,128)(2,1)S(1)}, bf16[48,2048]{1,0:T(8,128)(2,1)S(1)}, u32[]{:S(2)}, u32[]{:S(2)}) collective-permute-start(bf16[48,2048]{1,0:T(8,128)(2,1)S(1)} %add_convert_fusion.1.even), channel_id=1, source_target_pairs={{0,1},{1,0},{2,3},{3,2},{4,5},{5,4},{6,7},{7,6},{8,9},{9,8},{10,11... | collective-permute-start | bytes 589832 | tf_op jit(solution)/shard_map/ppermute | solution.py:236
  44.1 12.2 %collective-permute-start.4 = (bf16[48,2048]{1,0:T(8,128)(2,1)S(1)}, bf16[48,2048]{1,0:T(8,128)(2,1)S(1)}, u32[]{:S(2)}, u32[]{:S(2)}) collective-permute-start(bf16[48,2048]{1,0:T(8,128)(2,1)S(1)} %add_convert_fusion.1.even), channel_id=1, source_target_pairs={{0,2},{1,3},{2,0},{3,1},{4,6},{5,7},{6,4},{7,5},{8,10},{9,11},{10,... | collective-permute-start | bytes 589832 | tf_op jit(solution)/shard_map/ppermute | solution.py:236
  47.7 9.1 %collective-permute-start.22 = (bf16[32,2048]{1,0:T(8,128)(2,1)S(1)}, bf16[32,2048]{1,0:T(8,128)(2,1)S(1)}, u32[]{:S(2)}, u32[]{:S(2)}) collective-permute-start(bf16[32,2048]{1,0:T(8,128)(2,1)S(1)} %get-tuple-element.38), channel_id=1, source_target_pairs={{0,4},{4,0},{8,12},{12,8},{1,5},{5,1},{9,13},{13,9},{2,6},{6,2},{1... | collective-permute-start | bytes 393224 | tf_op jit(solution)/shard_map/ppermute | solution.py:236
  51.5 15.4 %collective-permute-start.11 = (bf16[48,2048]{1,0:T(8,128)(2,1)S(1)}, bf16[48,2048]{1,0:T(8,128)(2,1)S(1)}, u32[]{:S(2)}, u32[]{:S(2)}) collective-permute-start(bf16[48,2048]{1,0:T(8,128)(2,1)S(1)} %get-tuple-element.31), channel_id=1, source_target_pairs={{0,4},{4,0},{8,12},{12,8},{1,5},{5,1},{9,13},{13,9},{2,6},{6,2},{1... | collective-permute-start | bytes 589832 | tf_op jit(solution)/shard_map/ppermute | solution.py:236
  55.3 18.0 %collective-permute-start.3 = (bf16[48,2048]{1,0:T(8,128)(2,1)S(1)}, bf16[48,2048]{1,0:T(8,128)(2,1)S(1)}, u32[]{:S(2)}, u32[]{:S(2)}) collective-permute-start(bf16[48,2048]{1,0:T(8,128)(2,1)S(1)} %get-tuple-element.26), channel_id=1, source_target_pairs={{0,4},{4,0},{8,12},{12,8},{1,5},{5,1},{9,13},{13,9},{2,6},{6,2},{1... | collective-permute-start | bytes 589832 | tf_op jit(solution)/shard_map/ppermute | solution.py:236
  56.3 3.0 %collective-permute-start.13 = (bf16[48,2048]{1,0:T(8,128)(2,1)S(1)}, bf16[48,2048]{1,0:T(8,128)(2,1)S(1)}, u32[]{:S(2)}, u32[]{:S(2)}) collective-permute-start(bf16[48,2048]{1,0:T(8,128)(2,1)S(1)} %collective-permute-done.12.even), channel_id=1, source_target_pairs={{0,1},{1,0},{2,3},{3,2},{4,5},{5,4},{6,7},{7,6},{8,9},{9,8},{10,11... | collective-permute-start | bytes 589832 | tf_op jit(solution)/shard_map/ppermute | solution.py:236
  56.3 7.4 %collective-permute-start.5 = (bf16[48,2048]{1,0:T(8,128)(2,1)S(1)}, bf16[48,2048]{1,0:T(8,128)(2,1)S(1)}, u32[]{:S(2)}, u32[]{:S(2)}) collective-permute-start(bf16[48,2048]{1,0:T(8,128)(2,1)S(1)} %collective-permute-done.4.even), channel_id=1, source_target_pairs={{0,1},{1,0},{2,3},{3,2},{4,5},{5,4},{6,7},{7,6},{8,9},{9,8},{10,11... | collective-permute-start | bytes 589832 | tf_op jit(solution)/shard_map/ppermute | solution.py:236
  56.9 9.9 %collective-permute-start.23 = (bf16[32,2048]{1,0:T(8,128)(2,1)S(1)}, bf16[32,2048]{1,0:T(8,128)(2,1)S(1)}, u32[]{:S(2)}, u32[]{:S(2)}) collective-permute-start(bf16[32,2048]{1,0:T(8,128)(2,1)S(1)} %select_convert_fusion.2), channel_id=1, source_target_pairs={{0,8},{4,12},{8,0},{12,4},{1,9},{5,13},{9,1},{13,5},{2,10},{6,14},... | collective-permute-start | bytes 393224 | tf_op jit(solution)/shard_map/ppermute | solution.py:236
  62.0 8.0 %collective-permute-start.14 = (bf16[48,2048]{1,0:T(8,128)(2,1)S(1)}, bf16[48,2048]{1,0:T(8,128)(2,1)S(1)}, u32[]{:S(2)}, u32[]{:S(2)}) collective-permute-start(bf16[48,2048]{1,0:T(8,128)(2,1)S(1)} %get-tuple-element.33), channel_id=1, source_target_pairs={{0,4},{4,0},{8,12},{12,8},{1,5},{5,1},{9,13},{13,9},{2,6},{6,2},{1... | collective-permute-start | bytes 589832 | tf_op jit(solution)/shard_map/ppermute | solution.py:236
  66.4 9.9 %collective-permute-start.6 = (bf16[48,2048]{1,0:T(8,128)(2,1)S(1)}, bf16[48,2048]{1,0:T(8,128)(2,1)S(1)}, u32[]{:S(2)}, u32[]{:S(2)}) collective-permute-start(bf16[48,2048]{1,0:T(8,128)(2,1)S(1)} %get-tuple-element.28), channel_id=1, source_target_pairs={{0,4},{4,0},{8,12},{12,8},{1,5},{5,1},{9,13},{13,9},{2,6},{6,2},{1... | collective-permute-start | bytes 589832 | tf_op jit(solution)/shard_map/ppermute | solution.py:236
  70.1 16.1 %collective-permute-start.15 = (bf16[48,2048]{1,0:T(8,128)(2,1)S(1)}, bf16[48,2048]{1,0:T(8,128)(2,1)S(1)}, u32[]{:S(2)}, u32[]{:S(2)}) collective-permute-start(bf16[48,2048]{1,0:T(8,128)(2,1)S(1)} %select_convert_fusion), channel_id=1, source_target_pairs={{0,8},{4,12},{8,0},{12,4},{1,9},{5,13},{9,1},{13,5},{2,10},{6,14},... | collective-permute-start | bytes 589832 | tf_op jit(solution)/shard_map/ppermute | solution.py:236
  76.3 13.0 %collective-permute-start.7 = (bf16[48,2048]{1,0:T(8,128)(2,1)S(1)}, bf16[48,2048]{1,0:T(8,128)(2,1)S(1)}, u32[]{:S(2)}, u32[]{:S(2)}) collective-permute-start(bf16[48,2048]{1,0:T(8,128)(2,1)S(1)} %select_convert_fusion.1), channel_id=1, source_target_pairs={{0,8},{4,12},{8,0},{12,4},{1,9},{5,13},{9,1},{13,5},{2,10},{6,14},... | collective-permute-start | bytes 589832 | tf_op jit(solution)/shard_map/ppermute | solution.py:236
  (8 other events, 65.2 us)
